TPU v7x, 32 devices: a whole 2x2x4 slice. The times are simulated.
32 devices in a mesh: leaf: 4 (over z), row: 2 (over core), col: 4 (over y, x).
Axes of the slice: x: 2, y: 2, z: 4, core: 2. Of those that a mesh axis runs over, the one named last changes fastest.
Arguments:
- front_tiles: bfloat16 [4, 8, 4, 2, 128, 8, 4, 2, 128], P('leaf', None, None, 'row', None, None, 'col'), as said below
- regular: float32 [4, 8, 4, 2, 128], P('leaf', None, 'col', 'row'), may hold values from 0.25 to 2.5
- child_map: int32 [4, 62], P('leaf'), may hold values from 0 to 63, as said below
Outputs:
- panel_factor: float32 [4, 8, 4, 2, 128, 256], P('leaf', None, None, 'row', None, 'col')
- parent_update: float32 [4, 4, 4, 2, 128, 8, 4, 2, 128], P('leaf', None, None, 'row', None, None, 'col')
Inputs may be any that keep to these rules, and one draw needn't show every extreme that they name: Each leaf's front_tiles form a symmetric positive semidefinite matrix, the product of a block-sparse constraint matrix (2 of 16 variable blocks per block row), a positive diagonal and its transpose; blocks that share no variable block are zero. `child_map`: within a leaf the entries are strictly increasing.
All inputs are finite; a program needn't handle non-finite values.
Results may differ from a plain program's by a relative error of at most 0.0016.
Values may be sent and summed in bfloat16 or wider, within the bound.
No kernel may reach another device: no remote copies, remote signals or barrier semaphores. Data moves between devices by JAX's collectives and lax.ppermute only.
A program may use at most 128 MiB of HBM per device.

v0:
```python
import jax
import jax.numpy as jnp
from jax import lax
from jax.sharding import PartitionSpec as P

NPAN = 1


def broadcast(block, axis, source):
    block = jnp.where(lax.axis_index(axis) == source, block, jnp.zeros_like(block))
    return lax.psum(block, axis)


def passed_along(array, axis, by):
    length = lax.axis_size(axis)
    return lax.ppermute(array, axis, [(i, (i + by) % length) for i in range(length)])


def swapped(value, axis, bit):
    mask = 2**bit
    pairs = [(source, source ^ mask) for source in range(lax.axis_size(axis))]
    return lax.ppermute(value, axis, pairs)


def regularized(tiles, regular_local, col_at, row_at):
    shape = tiles.shape
    outer_ids = lax.broadcasted_iota(jnp.int32, shape, 0)
    col_ids = lax.broadcasted_iota(jnp.int32, shape, 1)
    cell_ids = lax.broadcasted_iota(jnp.int32, shape, 2)
    other_outer = lax.broadcasted_iota(jnp.int32, shape, 3)
    row_ids = lax.broadcasted_iota(jnp.int32, shape, 4)
    other_cell = lax.broadcasted_iota(jnp.int32, shape, 5)
    on_diagonal = (
        (outer_ids == other_outer)
        & (col_ids == col_at)
        & (row_ids == row_at)
        & (cell_ids == other_cell)
    )
    gains = regular_local[:, None, :, None, None, None]
    return tiles.astype(jnp.float32) + jnp.where(on_diagonal, gains, 0.0)


def shards(front_tiles, regular, child_map):
    row_count = lax.axis_size("row")
    col_count = lax.axis_size("col")
    row_at = lax.axis_index("row")
    col_at = lax.axis_index("col")
    tile_size = front_tiles.shape[-1]
    local_outer = front_tiles.shape[1]
    rows_local = local_outer * col_count * tile_size
    cols_local = local_outer * row_count * tile_size
    panel_width = row_count * tile_size
    highest = lax.Precision.HIGHEST
    front_six = front_tiles.reshape(
        local_outer, col_count, tile_size, local_outer, row_count, tile_size
    )
    regular_local = regular.reshape(local_outer, tile_size)
    local_panel = regularized(front_six[:, :, :, :1], regular_local, col_at, row_at).reshape(
        rows_local, panel_width
    )
    slab_cols = broadcast(local_panel, "col", 0)
    corner = lax.all_gather(slab_cols[0 * tile_size : 1 * tile_size], "row", axis=0, tiled=True)
    factor = jnp.linalg.cholesky(corner)
    solved = jax.scipy.linalg.solve_triangular(factor, slab_cols[tile_size:].T, lower=True).T
    own_rows = lax.dynamic_slice_in_dim(factor, row_at * tile_size, tile_size, 0)
    rows_part = jnp.concatenate(
        [jnp.zeros((0, panel_width), jnp.float32), own_rows, solved], axis=0
    )
    chosen = lax.dynamic_index_in_dim(
        rows_part.reshape(local_outer, col_count, tile_size, panel_width), col_at, 1, keepdims=False
    )
    cols_part = lax.all_gather(chosen[:, None], "row", axis=1, tiled=True).reshape(
        cols_local, panel_width
    )
    done = [(rows_part, cols_part)]
    all_panels = jnp.concatenate([pair[0] for pair in done], axis=1)
    all_cols = jnp.concatenate([pair[1] for pair in done], axis=1)
    schur_block = regularized(front_six, regular_local, col_at, row_at).reshape(
        rows_local, cols_local
    )
    schur_block = schur_block - jnp.einsum("ik,jk->ij", all_panels, all_cols, precision=highest)
    out_width = NPAN * panel_width // col_count
    factor_out = lax.dynamic_slice_in_dim(all_panels, col_at * out_width, out_width, 1)
    factor_out = factor_out.reshape(1, local_outer, col_count, 1, tile_size, out_width)
    targets = child_map.reshape(-1)
    child_blocks = targets.shape[0]
    panel_blocks = NPAN * row_count
    child_range = jnp.arange(child_blocks, dtype=jnp.int32)

    def source_of(parent_ids):
        matches = targets[None, :] == parent_ids[:, None]
        present = jnp.any(matches, axis=1)
        source_ids = panel_blocks + jnp.sum(jnp.where(matches, child_range[None, :], 0), axis=1)
        return (present, source_ids)

    low_block = schur_block.astype(jnp.bfloat16).reshape(1, rows_local, cols_local)
    every_rows = lax.all_gather(low_block, "row", axis=0, tiled=True)
    every_rows = every_rows.reshape(row_count * local_outer * col_count, tile_size, cols_local)
    outer_ids = jnp.arange(local_outer, dtype=jnp.int32)
    row_parents = (
        (outer_ids[:, None] * col_count + jnp.arange(col_count, dtype=jnp.int32)[None, :])
        * row_count
        + row_at
    ).reshape(-1)
    row_present, row_source = source_of(row_parents)
    row_index = (
        row_source % row_count * (local_outer * col_count)
        + row_source // (row_count * col_count) * col_count
        + row_source // row_count % col_count
    )
    row_index = jnp.where(row_present, row_index, 0)
    routed_rows = jnp.take(every_rows, row_index, axis=0)
    routed_rows = jnp.where(row_present[:, None, None], routed_rows, jnp.zeros_like(routed_rows))
    routed_rows = routed_rows.reshape(rows_local, local_outer * row_count, tile_size)
    candidates = [routed_rows]
    candidates.append(passed_along(routed_rows, "col", -1))
    stacked = jnp.concatenate(candidates, axis=1)
    col_parents = (
        (outer_ids[:, None] * col_count + col_at) * row_count
        + jnp.arange(row_count, dtype=jnp.int32)[None, :]
    ).reshape(-1)
    col_present, col_source = source_of(col_parents)
    reach_ids = col_source // row_count - col_parents // row_count
    col_index = (
        reach_ids * (local_outer * row_count)
        + col_source // (row_count * col_count) * row_count
        + col_source % row_count
    )
    col_index = jnp.where(col_present, col_index, 0)
    routed = jnp.take(stacked, col_index, axis=1)
    routed = jnp.where(col_present[None, :, None], routed, jnp.zeros_like(routed))
    routed = routed.reshape(local_outer, col_count, tile_size, cols_local)
    half_outer = local_outer // 2
    leaf_side = lax.axis_index("leaf") % 2
    kept_rows = lax.dynamic_slice_in_dim(routed, leaf_side * half_outer, half_outer, 0)
    sent_rows = lax.dynamic_slice_in_dim(routed, (1 - leaf_side) * half_outer, half_outer, 0)
    partner_rows = swapped(sent_rows, "leaf", 0)
    merged = kept_rows.astype(jnp.float32) + partner_rows.astype(jnp.float32)
    merged = merged.reshape(
        1, half_outer, col_count, 1, tile_size, local_outer, 1, row_count, tile_size
    )
    return (factor_out, merged)


def solution(mesh):
    return jax.shard_map(
        shards,
        mesh=mesh,
        in_specs=(
            P("leaf", None, None, "row", None, None, "col", None, None),
            P("leaf", None, "col", "row", None),
            P("leaf", None),
        ),
        out_specs=(
            P("leaf", None, None, "row", None, "col"),
            P("leaf", None, None, "row", None, None, "col", None, None),
        ),
        check_vma=False,
    )
```

profile of v0, /device:TPU:0, one launch (start us, length us, event | category | flops | bytes accessed | tf_op | source)
XLA Modules:
  0.0 1118.3 jit_solution(5900588107595066955)
XLA Ops:
  7.3 4.9 fusion.1
  12.2 2.3 copy.44
  14.5 5.6 copy.37
  20.2 106.6 %all-reduce.3.cloned.1.call-done = f32[4096,256]{0,1:T(8,128)} async-done(((f32[4096,256]{0,1:T(8,128)}), f32[4096,256]{0,1:T(8,128)}) %all-reduce.3.cloned.1.call-update) | async-done | bytes 4194320 | tf_op jit(solution)/shard_map/psum | solution.py:11
  126.9 0.9 slice.75
  127.8 2.0 all_gather.9
  130.0 11.7 %cholesky.50 = f32[128,128]{1,0:T(8,128)S(1)} custom-call(f32[128,128]{1,0:T(8,128)S(1)} %cholesky.118), custom_call_target="Cholesky" | custom-call | tf_op jit(solution)/shard_map/jit(cholesky)/cholesky | solution.py:63
  141.7 9.8 custom-call.15
  152.0 11.7 %cholesky.105 = f32[128,128]{1,0:T(8,128)S(1)} custom-call(f32[128,128]{1,0:T(8,128)S(1)} %convolution_subtract_fusion.1), custom_call_target="Cholesky" | custom-call | tf_op jit(solution)/shard_map/jit(cholesky)/cholesky | solution.py:63
  163.8 0.7 compare_reduce_fusion.2
  165.8 4.2 while.1
  166.1 0.6 fusion.37
  166.7 1.4 bitcast_dynamic-update-slice_fusion.2
  168.6 1.4 bitcast_dynamic-update-slice_fusion.2
  170.0 19.7 %custom-call.16 = f32[2,128,128]{1,2,0:T(8,128)S(1)} custom-call(f32[2,128,128]{2,1,0:T(8,128)S(1)} %get-tuple-element.9), custom_call_target="InvertDiagBlocksLowerTriangular" | custom-call | tf_op jit(solution)/shard_map/jit(_solve_triangular)/triangular_solve | solution.py:64
  189.7 2.4 slice_bitcast_fusion
  192.1 1.9 fusion.2
  194.0 1.9 convolution_subtract_fusion
  195.8 1.9 fusion.8
  197.7 2.2 maximum_bitcast_fusion
  200.1 4.6 pad_maximum_fusion.1
  204.7 6.0 reshape.524
  210.7 3.3 constant_dynamic-slice_fusion.1
  214.0 2.1 copy.40
  216.2 28.8 %reshape.548 = f32[4096,2048]{1,0:T(8,128)} reshape(bf16[1,8,4,1,128,8,1,2,128]{8,7,6,5,4,3,2,1,0:T(2,128)(2,1)} %param.3) | data formatting | bytes 50331648 | tf_op jit(solution)/shard_map/convert_element_type | solution.py:40
  245.1 4.7 pad_maximum_fusion.5
  249.8 1.8 copy.33
  251.7 72.8 %subtract_convert_fusion = bf16[4096,2048]{1,0:T(8,128)(2,1)} fusion(f32[4096,2048]{1,0:T(8,128)} %reshape.548, f32[4096]{0:T(1024)S(1)} %bitcast.132, s32[2048]{0:T(1024)S(1)} %bitcast.135, s32[2048]{0:T(1024)S(1)} %bitcast.136, s32[4096]{0:T(1024)S(1)} %bitcast.133, s32[4096]{0:T(1024)S(1)} %bitcast.134, pred[4096]{0:T(1024)(128)(4,1)S(1)} %bitcast.137, ...), kind=kOutput, calls=%fused_computation.5 | convolution fusion | flops 25845301248 | bytes 56694784 | tf_op jit(solution)/shard_map/ik,jk->ij/dot_general | solution.py:81
  325.6 50.3 %all-gather.6.cloned.1.call-done = bf16[8192,2048]{1,0:T(8,128)(2,1)} async-done(((bf16[4096,2048]{1,0:T(8,128)(2,1)}), bf16[8192,2048]{1,0:T(8,128)(2,1)}) %all-gather.6.cloned.1.call-update) | async-done | bytes 33554448 | tf_op jit(solution)/shard_map/all_gather | solution.py:97
  375.9 11.9 %gather_fusion = bf16[32,128,2048]{2,1,0:T(8,128)(2,1)} fusion(bf16[64,128,2048]{2,1,0:T(8,128)(2,1)} %bitcast.128, s32[1024]{0:T(1024)S(1)} %pad_clamp_fusion.1), kind=kCustom, calls=%fused_computation | custom fusion | bytes 33554560 | tf_op jit(solution)/shard_map/jit(_take)/gather | solution.py:112
  387.8 15.1 %copy.42 = bf16[512,8,16,128]{3,2,1,0:T(8,128)(2,1)} copy(bf16[512,8,16,128]{3,1,2,0:T(8,128)(2,1)} %bitcast.122) | data formatting | bytes 33554432
  402.9 22.4 %copy.38 = bf16[4096,16,128]{0,2,1:T(8,128)(2,1)} copy(bf16[4096,16,128]{2,1,0:T(8,128)(2,1)} %bitcast.124) | data formatting | bytes 33554432 | tf_op jit(solution)/shard_map/jit(_take)/gather | solution.py:112
  425.3 14.1 %select_select_fusion.1 = bf16[4096,16,128]{0,2,1:T(8,128)(2,1)} fusion(bf16[4096,16,128]{0,2,1:T(8,128)(2,1)} %copy.38, pred[4096]{0:T(1024)(128)(4,1)S(1)} %get-tuple-element.38, pred[4096]{0:T(1024)(128)(4,1)S(1)} %get-tuple-element.39), kind=kLoop, calls=%fused_computation.8 | loop fusion | flops 16777216 | bytes 33562624 | tf_op jit(solution)/shard_map/jit(_where)/select_n | solution.py:113
  439.4 2.6 collective-permute-start
  442.8 359.5 %collective-permute-done = bf16[4096,16,128]{0,2,1:T(8,128)(2,1)} collective-permute-done((bf16[4096,16,128]{0,2,1:T(8,128)(2,1)}, bf16[4096,16,128]{0,2,1:T(8,128)(2,1)}, u32[]{:S(2)}, u32[]{:S(2)}) %collective-permute-start) | collective-permute-done | bytes 16777248 | tf_op jit(solution)/shard_map/ppermute | solution.py:16
  802.3 22.8 %pad_maximum_fusion = bf16[4096,32,128]{0,2,1:T(8,128)(2,1)} fusion(bf16[4096,16,128]{0,2,1:T(8,128)(2,1)} %collective-permute-done, bf16[4096,16,128]{0,2,1:T(8,128)(2,1)} %select_select_fusion.1), kind=kLoop, calls=%fused_computation.4 | loop fusion | flops 16777216 | bytes 67108864 | tf_op jit(solution)/shard_map/concatenate | solution.py:117
  825.1 12.0 %gather_fusion.1 = bf16[16,4096,128]{1,2,0:T(8,128)(2,1)} fusion(bf16[4096,32,128]{0,2,1:T(8,128)(2,1)} %pad_maximum_fusion, s32[1024]{0:T(1024)S(1)} %pad_clamp_fusion), kind=kCustom, calls=%fused_computation.1 | custom fusion | bytes 33554496 | tf_op jit(solution)/shard_map/jit(_take)/gather | solution.py:130
  837.1 27.3 %gather.18 = bf16[8,4,128,2048]{2,1,0,3:T(4,128)(2,1)} reshape(bf16[4096,16,128]{0,2,1:T(8,128)(2,1)} %bitcast.123) | data formatting | bytes 33554432 | tf_op jit(solution)/shard_map/jit(_take)/gather | solution.py:130
  864.4 16.4 %select_select_fusion = bf16[8,4,128,2048]{2,1,0,3:T(4,128)(2,1)S(1)} fusion(bf16[8,4,128,2048]{2,1,0,3:T(4,128)(2,1)} %gather.18, pred[2048]{0:T(1024)(128)(4,1)S(1)} %get-tuple-element.40, pred[2048]{0:T(1024)(128)(4,1)S(1)} %get-tuple-element.41), kind=kLoop, calls=%fused_computation.7 | loop fusion | flops 16777216 | bytes 33558528 | tf_op jit(solution)/shard_map/jit(_where)/select_n | solution.py:131
  880.8 6.5 constant_dynamic-slice_fusion.2
  887.3 2.2 copy-done
  889.5 1.6 collective-permute-start.1
  891.1 1.3 fusion.4
  892.4 0.7 reshape.523
  893.1 1.6 copy.36
  894.7 177.0 %collective-permute-done.1 = bf16[4,4,128,2048]{2,1,0,3:T(4,128)(2,1)} collective-permute-done((bf16[4,4,128,2048]{2,1,0,3:T(4,128)(2,1)}, bf16[4,4,128,2048]{2,1,0,3:T(4,128)(2,1)}, u32[]{:S(2)}, u32[]{:S(2)}) %collective-permute-start.1) | collective-permute-done | bytes 8388640 | tf_op jit(solution)/shard_map/ppermute | solution.py:22
  1071.6 15.0 %convert_add_fusion = f32[4,4,128,2048]{2,1,0,3:T(4,128)} fusion(bf16[4,4,128,2048]{2,1,0,3:T(4,128)(2,1)} %collective-permute-done.1, bf16[8,4,128,2048]{2,1,0,3:T(4,128)(2,1)} %copy-done, s32[]{:T(128)S(6)} %select_n.306), kind=kLoop, calls=%fused_computation.6 | loop fusion | flops 12582912 | bytes 33554436 | tf_op jit(solution)/shard_map/add | solution.py:138
  1086.6 24.9 %copy.39 = f32[1,4,4,1,128,8,1,2,128]{8,7,6,5,4,3,2,1,0:T(2,128)} copy(f32[1,4,4,1,128,8,1,2,128]{4,2,1,8,7,5,6,3,0:T(4,128)} %bitcast.121) | data formatting | bytes 33554432 | tf_op jit(solution)/shard_map/reshape | solution.py:139
  (59 shorter events, 3.8 us)
Async XLA Ops:
  7.2 119.7 %all-reduce.3.cloned.1.call-start = ((), (), s32[]{:S(2)}) async-start(), calls=%async_computation | async-start | bytes 8388608 | tf_op jit(solution)/shard_map/psum | solution.py:11
  20.2 229.6 %all-gather.4.cloned.1.call-start = ((), (), s32[]{:S(2)}) async-start(), calls=%async_computation.1 | async-start | bytes 3145728 | tf_op jit(solution)/shard_map/all_gather | solution.py:72
  216.1 159.8 %all-gather.6.cloned.1.call-start = ((), (), s32[]{:S(2)}) async-start(), calls=%async_computation.2 | async-start | bytes 50331648 | tf_op jit(solution)/shard_map/all_gather | solution.py:97
  245.0 6.5 copy-start.1
  324.4 0.7 copy-start.2
  439.4 362.9 %collective-permute-start = (bf16[4096,16,128]{0,2,1:T(8,128)(2,1)}, bf16[4096,16,128]{0,2,1:T(8,128)(2,1)}, u32[]{:S(2)}, u32[]{:S(2)}) collective-permute-start(bf16[4096,16,128]{0,2,1:T(8,128)(2,1)} %select_select_fusion.1), channel_id=1, source_target_pairs={{0,3},{1,0},{2,1},{3,2},{4,7},{5,4},{6,5},{7,6},{8,11},{9,8},{10,9... | collective-permute-start | bytes 50331656 | tf_op jit(solution)/shard_map/ppermute | solution.py:16
  880.8 8.7 copy-start
  889.5 182.2 %collective-permute-start.1 = (bf16[4,4,128,2048]{2,1,0,3:T(4,128)(2,1)}, bf16[4,4,128,2048]{2,1,0,3:T(4,128)(2,1)}, u32[]{:S(2)}, u32[]{:S(2)}) collective-permute-start(bf16[4,4,128,2048]{2,1,0,3:T(4,128)(2,1)} %constant_dynamic-slice_fusion.2), channel_id=1, source_target_pairs={{0,8},{8,0},{16,24},{24,16},{1,9},{9,1},{17,25},{25,17},{2,10},{10... | collective-permute-start | bytes 25165832 | tf_op jit(solution)/shard_map/ppermute | solution.py:22
Sparse Core Ops, SparseCore 0:
  20.3 106.5 all-reduce.2
  216.2 10.5 all-gather.3
  324.6 51.2 all-gather.5
where the time goes:
time: 1130 us; the launch traced here: 1120 us
  waiting for transfers between devices  693 us (61%)
  local copies, waits for them, and re-layouts  183 us (16%)
  other arithmetic  141 us (12%)
  matrix products  78.8 us (7%)
  between operations  15.6 us (1%)
    ppermute x1, waiting for transfers between devices, passed_along(): lax.ppermute(array, axis, [(i, (i + by) % length) for i in range(length)])  360 us
    ppermute x1, waiting for transfers between devices, swapped(): return lax.ppermute(value, axis, pairs)  177 us
    psum x1, waiting for transfers between devices, broadcast(): return lax.psum(block, axis)  107 us
    dot_general x1, matrix products, shards(): jnp.einsum('ik,jk->ij', all_panels, all_cols, precision=highest)  72.8 us
    all_gather x1, waiting for transfers between devices, shards(): every_rows = lax.all_gather(low_block, 'row', axis=0, tiled=True)  50.3 us
    gather x2, local copies, waits for them, and re-layouts, shards(): routed = jnp.take(stacked, col_index, axis=1)  39.3 us
    gather x2, local copies, waits for them, and re-layouts, shards(): routed_rows = jnp.take(every_rows, row_index, axis=0)  34.3 us
    another operation x6, other arithmetic, shards(): factor = jnp.linalg.cholesky(corner)  34 us
  transfers between devices with their start and end apart: 5, of which 4 were waited for; matrix products, arithmetic and copies ran while one was open for 3% of the time, Pallas kernels for 0%

commit v1 on v0

v1 whole, which is shorter than its diff:
```python
import functools

import jax
import jax.numpy as jnp
from jax import lax
from jax.experimental import pallas as pl
from jax.experimental.pallas import tpu as pltpu
from jax.sharding import PartitionSpec as P

NPAN = 1
VMEM_LIMIT = 60 * 1024 * 1024
CLASSES = 5
f32 = jnp.float32
bf16 = jnp.bfloat16
i32 = jnp.int32
HIGHEST = lax.Precision.HIGHEST


def untangle_kernel(tile, ncols, x_ref, out_ref, wide):
    wide[...] = x_ref[...].astype(f32)
    for j in range(ncols):
        out_ref[j] = wide[pl.ds(j, tile, stride=ncols), :].astype(bf16)


def untangled(x, tile, ncols):
    count = x.shape[0] // (tile * ncols)
    return pl.pallas_call(
        functools.partial(untangle_kernel, tile, ncols),
        out_shape=jax.ShapeDtypeStruct((count, ncols, tile, tile), bf16),
        scratch_shapes=[pltpu.VMEM((tile * ncols, tile), f32)],
        grid=(count,),
        in_specs=[pl.BlockSpec((tile * ncols, tile), lambda i: (i, 0))],
        out_specs=pl.BlockSpec((None, ncols, tile, tile), lambda i: (i, 0, 0, 0)),
        name="untangle",
    )(x)


def sort_kernel(dims, parent_ref, where_ref, x_ref, *rest):
    tile, nrows, ncols, rows, cols, cap = dims
    bufs = rest[:CLASSES]
    metas = rest[CLASSES : 2 * CLASSES]
    over_ref = rest[2 * CLASSES]
    wide, blocks, seen, found_v, found, counts, sem, found_sem = rest[2 * CLASSES + 1 :]
    step = pl.program_id(0)
    wide[...] = x_ref[...].astype(f32)
    for j in range(ncols):
        block = wide[pl.ds(j, tile, stride=ncols), :]
        at = step * ncols + j
        blocks[at] = block.astype(bf16)
        top = jnp.max(jnp.abs(block), axis=0, keepdims=True)
        seen[pl.ds(at, 1), :] = jnp.where(top > 0, 1.0, 0.0)

    @pl.when(step == nrows - 1)
    def _():
        hits = lax.dot_general(
            jnp.ones((8, tile), f32),
            seen[...],
            (((1,), (1,)), ((), ())),
            preferred_element_type=f32,
        )
        found_v[...] = hits.astype(i32)
        copy = pltpu.make_async_copy(found_v, found, found_sem)
        copy.start()
        side = where_ref[0]
        row_at = where_ref[1]
        col_at = where_ref[2]
        half = nrows * rows // 2
        for k in range(CLASSES):
            counts[k] = 0
        copy.wait()

        def one_row(i, carry):
            parent_row = parent_ref[i * rows + row_at]

            @pl.when(parent_row >= 0)
            def _():
                moves_leaf = parent_row // half != side
                target_row = parent_row % rows
                moves_row = target_row != row_at
                place_row = parent_row // rows % (nrows // 2)

                def one_col(j, inner):
                    source_col = ((j // rows) * cols + col_at) * rows + j % rows
                    parent_col = parent_ref[source_col]

                    @pl.when((found[0, i * ncols + j] > 0) & (parent_col >= 0))
                    def _():
                        moves_col = parent_col // rows % cols != col_at
                        place_col = parent_col // (rows * cols) * rows + parent_col % rows
                        kind = jnp.where(
                            moves_leaf,
                            jnp.where(moves_col, 4, 3),
                            jnp.where(moves_col, 2, jnp.where(moves_row, 1, 0)),
                        )
                        slot = counts[kind]
                        counts[kind] = slot + 1
                        code = (place_row * ncols + place_col) * rows + target_row
                        for k in range(CLASSES):

                            @pl.when((kind == k) & (slot < cap))
                            def _():
                                metas[k][1 + slot] = code
                                pltpu.make_async_copy(
                                    blocks.at[i * ncols + j], bufs[k].at[slot], sem
                                ).start()

                    return inner

                lax.fori_loop(0, ncols, one_col, 0)

            return carry

        lax.fori_loop(0, nrows, one_row, 0)
        sent = 0
        over = 0
        for k in range(CLASSES):
            taken = jnp.minimum(counts[k], cap)
            metas[k][0] = taken
            sent = sent + taken
            over = over + (counts[k] - taken)
        over_ref[0] = over

        def drain(_, carry):
            pltpu.make_async_copy(blocks.at[0], bufs[0].at[0], sem).wait()
            return carry

        lax.fori_loop(0, sent, drain, 0)


def sorted_blocks(x, parent, where, dims):
    tile, nrows, ncols, rows, cols, cap = dims
    count = nrows * ncols
    smem = pl.BlockSpec(memory_space=pltpu.SMEM)
    return pl.pallas_call(
        functools.partial(sort_kernel, dims),
        out_shape=[jax.ShapeDtypeStruct((cap, tile, tile), bf16)] * CLASSES
        + [jax.ShapeDtypeStruct((cap + 8,), i32)] * CLASSES
        + [jax.ShapeDtypeStruct((1,), i32)],
        grid=(nrows,),
        in_specs=[smem, smem, pl.BlockSpec((tile * ncols, tile), lambda i: (i, 0))],
        out_specs=[pl.BlockSpec(memory_space=pl.ANY)] * CLASSES + [smem] * (CLASSES + 1),
        scratch_shapes=[
            pltpu.VMEM((tile * ncols, tile), f32),
            pltpu.VMEM((count, tile, tile), bf16),
            pltpu.VMEM((count, tile), f32),
            pltpu.VMEM((8, count), i32),
            pltpu.SMEM((8, count), i32),
            pltpu.SMEM((CLASSES,), i32),
            pltpu.SemaphoreType.DMA,
            pltpu.SemaphoreType.DMA,
        ],
        compiler_params=pltpu.CompilerParams(vmem_limit_bytes=VMEM_LIMIT),
        name="sort_blocks",
    )(parent, where, x)


def eliminate(work, tile):
    rows = lax.broadcasted_iota(i32, (tile, tile), 0)
    lanes = lax.broadcasted_iota(i32, (tile, tile), 1)

    def one(k, carry):
        for leaf in range(2):
            left = work[leaf, :, :tile]
            pivot_row = work[leaf, pl.ds(k, 1), :]
            column = jnp.sum(jnp.where(lanes == k, left, 0.0), axis=1, keepdims=True)
            lane_row = lax.broadcasted_iota(i32, (1, tile), 1)
            pivot = jnp.sum(
                jnp.where(lane_row == k, pivot_row[:, :tile], 0.0), axis=1, keepdims=True
            )
            ratio = jnp.where(rows[:, :1] > k, column / pivot, 0.0)
            work[leaf] = work[leaf] - ratio * pivot_row
        return carry

    lax.fori_loop(0, tile, one, 0)


def full_dot(a, b):
    return jnp.dot(a, b, precision=HIGHEST, preferred_element_type=f32)


def corner_kernel(tile, corner_ref, reg_ref, inverse_ref, upper_ref, work):
    rows = lax.broadcasted_iota(i32, (tile, tile), 0)
    lanes = lax.broadcasted_iota(i32, (tile, tile), 1)
    eye = jnp.where(rows == lanes, 1.0, 0.0).astype(f32)

    def block(leaf, i, j):
        value = corner_ref[i, leaf, j].astype(f32)
        if i == j:
            value = value + jnp.where(rows == lanes, reg_ref[i, leaf], 0.0)
        return value

    def finish(leaf):
        upper = work[leaf, :, :tile]
        unit = work[leaf, :, tile:]
        pivots = jnp.sum(jnp.where(rows == lanes, upper, 0.0), axis=1, keepdims=True)
        scale = 1.0 / jnp.sqrt(pivots)
        return jnp.where(lanes >= rows, upper * scale, 0.0), jnp.where(
            lanes <= rows, unit * scale, 0.0
        )

    for leaf in range(2):
        work[leaf, :, :tile] = block(leaf, 0, 0)
        work[leaf, :, tile:] = eye
    eliminate(work, tile)
    for leaf in range(2):
        upper, inverse = finish(leaf)
        cross = full_dot(inverse, block(leaf, 0, 1))
        upper_ref[leaf, :tile, :tile] = upper
        upper_ref[leaf, :tile, tile:] = cross
        upper_ref[leaf, tile:, :tile] = jnp.zeros((tile, tile), f32)
        inverse_ref[leaf, :tile, :tile] = inverse
        inverse_ref[leaf, :tile, tile:] = jnp.zeros((tile, tile), f32)
        work[leaf, :, :tile] = block(leaf, 1, 1) - full_dot(cross.T, cross)
        work[leaf, :, tile:] = eye
    eliminate(work, tile)
    for leaf in range(2):
        upper, inverse = finish(leaf)
        cross = upper_ref[leaf, :tile, tile:]
        upper_ref[leaf, tile:, tile:] = upper
        inverse_ref[leaf, tile:, tile:] = inverse
        low = full_dot(cross.T, inverse_ref[leaf, :tile, :tile])
        inverse_ref[leaf, tile:, :tile] = -full_dot(inverse, low)


def corner_factors(corner, reg, tile):
    wide = jax.ShapeDtypeStruct((2, 2 * tile, 2 * tile), f32)
    return pl.pallas_call(
        functools.partial(corner_kernel, tile),
        out_shape=[wide, wide],
        scratch_shapes=[pltpu.VMEM((2, tile, 2 * tile), f32)],
        name="corner_factors",
    )(corner, reg)


def split3(x):
    high = x.astype(bf16)
    rest = x - high.astype(f32)
    mid = rest.astype(bf16)
    low = (rest - mid.astype(f32)).astype(bf16)
    return high, mid, low


def solve_kernel(dims, source_ref, where_ref, inverse_ref, upper_ref, panel_ref, *rest):
    tile, nrows, ncols, rows, cols, width = dims
    factor_ref, left_ref, right_ref = rest
    row_at = where_ref[1]
    col_at = where_ref[2]
    half = nrows * rows // 2
    side = where_ref[0]

    def raw(leaf, block):
        at = block // rows % cols
        j = block // (rows * cols) * rows + block % rows
        return jnp.concatenate([panel_ref[s * cols + at, leaf, j] for s in range(rows)], axis=0)

    def dots(pieces, value):
        total = jnp.dot(pieces[0], value, preferred_element_type=f32)
        for piece in pieces[1:]:
            total = total + jnp.dot(piece, value, preferred_element_type=f32)
        return total

    own = split3(inverse_ref[0, pl.ds(pl.multiple_of(col_at * width, width), width), :])

    def factor(i, carry):
        factor_ref[i] = dots(own, raw(0, i * rows + row_at))
        return carry

    lax.fori_loop(1, nrows, factor, 0)
    top = upper_ref[0, pl.ds(pl.multiple_of(col_at * width, width), width), :]
    factor_ref[0] = jnp.where(row_at == 0, top[:, :tile], top[:, tile:])
    for leaf in range(2):
        pieces = split3(inverse_ref[leaf])

        def solved(block):
            value = dots(pieces, raw(leaf, jnp.maximum(block, 0)))
            return jnp.where(block >= 0, value, 0.0)

        for j in range(ncols):
            parent = ((j // rows) * cols + col_at) * rows + j % rows
            value = solved(source_ref[leaf, parent])
            high = value.astype(bf16)
            low = (value - high.astype(f32)).astype(bf16)
            depth = rows * tile
            lanes = pl.ds(j * tile, tile)
            right_ref[leaf, :depth, lanes] = high
            right_ref[leaf, depth : 2 * depth, lanes] = low
            right_ref[leaf, 2 * depth :, lanes] = high

        def left(i, carry):
            parent = side * half + i * rows + row_at
            value = solved(source_ref[leaf, parent]).T
            high = value.astype(bf16)
            low = (value - high.astype(f32)).astype(bf16)
            left_ref[leaf, i] = jnp.concatenate([high, high, low], axis=1)
            return carry

        lax.fori_loop(0, nrows // 2, left, 0)


def solved_panels(source, where, inverse, upper, panel, dims):
    tile, nrows, ncols, rows, cols, width = dims
    smem = pl.BlockSpec(memory_space=pltpu.SMEM)
    vmem = pl.BlockSpec(memory_space=pltpu.VMEM)
    depth = 3 * rows * tile
    return pl.pallas_call(
        functools.partial(solve_kernel, dims),
        out_shape=[
            jax.ShapeDtypeStruct((nrows, width, tile), f32),
            jax.ShapeDtypeStruct((2, nrows // 2, tile, depth), bf16),
            jax.ShapeDtypeStruct((2, depth, ncols * tile), bf16),
        ],
        in_specs=[smem, smem, vmem, vmem, vmem],
        out_specs=[vmem, vmem, vmem],
        compiler_params=pltpu.CompilerParams(vmem_limit_bytes=VMEM_LIMIT),
        name="solve_panels",
    )(source, where, inverse, upper, panel)


def merge_kernel(dims, leaves, source_ref, where_ref, *rest):
    tile, nrows, ncols, rows, cols, group = dims
    count = len(leaves)
    metas = rest[:count]
    bufs = rest[count : 2 * count]
    reg_ref, left_ref, right_ref, out_ref = rest[2 * count : 2 * count + 4]
    table, blocks, totals, sem = rest[2 * count + 4 :]
    step = pl.program_id(0)
    side = where_ref[0]
    row_at = where_ref[1]
    col_at = where_ref[2]
    half = nrows * rows // 2
    per_leaf = nrows // 2 * ncols

    @pl.when(step == 0)
    def _():
        def clear(i, carry):
            table[i] = 0
            return carry

        lax.fori_loop(0, 2 * per_leaf, clear, 0)
        blocks[0] = jnp.zeros((tile, tile), bf16)
        filled = 1
        for k in range(count):

            def place(e, slot):
                code = metas[k][1 + e]
                mine = code % rows == row_at

                @pl.when(mine)
                def _():
                    table[leaves[k] * per_leaf + code // rows] = slot
                    pltpu.make_async_copy(bufs[k].at[e], blocks.at[slot], sem).start()

                return slot + jnp.where(mine, 1, 0)

            filled = lax.fori_loop(0, metas[k][0], place, filled)

        def drain(_, carry):
            pltpu.make_async_copy(bufs[0].at[0], blocks.at[0], sem).wait()
            return carry

        lax.fori_loop(1, filled, drain, 0)

    for leaf in range(2):
        left = left_ref[leaf].reshape(group * tile, left_ref.shape[-1])
        totals[leaf] = jnp.dot(left, right_ref[leaf], preferred_element_type=f32)
    on_diagonal = lax.broadcasted_iota(i32, (tile, tile), 0) == lax.broadcasted_iota(
        i32, (tile, tile), 1
    )
    for g in range(group):
        place_row = step * group + g
        parent = side * half + place_row * rows + row_at

        @pl.when(parent // rows % cols == col_at)
        def _():
            j = parent // (rows * cols) * rows + parent % rows
            lanes = pl.ds(pl.multiple_of(j * tile, tile), tile)
            for leaf in range(2):
                block = source_ref[leaf, parent]

                @pl.when(block >= 0)
                def _():
                    at = (block % rows * cols + block // rows % cols) * 2 + leaf
                    gain = reg_ref[at, pl.ds(block // (rows * cols), 1), :]
                    here = totals[leaf, g * tile : (g + 1) * tile, lanes]
                    totals[leaf, g * tile : (g + 1) * tile, lanes] = here - jnp.where(
                        on_diagonal, gain, 0.0
                    )

        for j in range(ncols):
            parts = []
            for leaf in range(2):
                slot = table[leaf * per_leaf + place_row * ncols + j]
                total = totals[leaf, g * tile : (g + 1) * tile, j * tile : (j + 1) * tile]
                parts.append((blocks[slot].astype(f32) - total).astype(bf16).astype(f32))
            out_ref[pl.ds(g * tile * ncols + j, tile, stride=ncols), :] = parts[0] + parts[1]


def merged_parent(source, where, metas, bufs, leaves, reg, left, right, dims):
    tile, nrows, ncols, rows, cols, group = dims
    count = len(leaves)
    smem = pl.BlockSpec(memory_space=pltpu.SMEM)
    hbm = pl.BlockSpec(memory_space=pl.ANY)
    vmem = pl.BlockSpec(memory_space=pltpu.VMEM)
    depth = left.shape[-1]
    return pl.pallas_call(
        functools.partial(merge_kernel, dims, leaves),
        out_shape=jax.ShapeDtypeStruct((nrows // 2 * tile * ncols, tile), f32),
        grid=(nrows // 2 // group,),
        in_specs=[smem] * (2 + count)
        + [hbm] * count
        + [
            vmem,
            pl.BlockSpec((2, group, tile, depth), lambda i: (0, i, 0, 0)),
            vmem,
        ],
        out_specs=pl.BlockSpec((group * tile * ncols, tile), lambda i: (i, 0)),
        scratch_shapes=[
            pltpu.SMEM((nrows * ncols,), i32),
            pltpu.VMEM((nrows * ncols + 1, tile, tile), bf16),
            pltpu.VMEM((2, group * tile, ncols * tile), f32),
            pltpu.SemaphoreType.DMA,
        ],
        compiler_params=pltpu.CompilerParams(vmem_limit_bytes=VMEM_LIMIT),
        name="merge_parent",
    )(source, where, *metas, *bufs, reg, left, right)


def sparse_sources(child_map, blocks, panel_blocks):
    targets = child_map[:, None, :]
    matches = targets == jnp.arange(blocks, dtype=i32)[None, :, None]
    ids = panel_blocks + jnp.arange(child_map.shape[1], dtype=i32)
    return jnp.sum(jnp.where(matches, ids + 1, 0), axis=2) - 1


def shards(front_tiles, regular, child_map):
    rows = lax.axis_size("row")
    cols = lax.axis_size("col")
    leaves = lax.axis_size("leaf")
    row_at = lax.axis_index("row")
    col_at = lax.axis_index("col")
    side = lax.axis_index("leaf") % 2
    tile = front_tiles.shape[-1]
    outer = front_tiles.shape[1]
    nrows = outer * cols
    ncols = outer * rows
    blocks = nrows * rows
    cap = nrows * ncols * 5 // 32
    width = NPAN * rows * tile // cols
    group = 2
    where = jnp.stack([side, row_at, col_at]).astype(i32)
    flat = front_tiles.reshape(nrows * tile * ncols, tile)
    leaf_pairs = [(i, i ^ 1) for i in range(leaves)]
    col_pairs = [(i, (i - 1) % cols) for i in range(cols)]
    row_pairs = [(i, (i + 1) % rows) for i in range(rows)]
    both_pairs = [
        (i * cols + j, (i ^ 1) * cols + (j - 1) % cols)
        for i in range(leaves)
        for j in range(cols)
    ]

    own_panel = untangled(flat[: tile * ncols], tile, ncols)[0]
    own_small = jnp.concatenate(
        [regular.reshape(-1), child_map.reshape(-1).astype(f32)]
    )
    sib_panel = lax.ppermute(own_panel, "leaf", leaf_pairs)
    sib_small = lax.ppermute(own_small, "leaf", leaf_pairs)
    panel = lax.all_gather(jnp.stack([own_panel, sib_panel]), ("row", "col"))
    gains = jnp.stack([own_small[: outer * tile], sib_small[: outer * tile]])
    reg = lax.all_gather(gains, ("row", "col"))
    reg = reg.reshape(rows * cols, 2, outer, tile)
    maps = jnp.stack([child_map.reshape(-1), sib_small[outer * tile :].astype(i32)])
    source = sparse_sources(maps, blocks, NPAN * rows)

    parent = jnp.concatenate([jnp.full((NPAN * rows,), -1, i32), child_map.reshape(-1)])
    *found, over = sorted_blocks(flat, parent, where, (tile, nrows, ncols, rows, cols, cap))
    kept, row_move, col_move, leaf_move, far_move = found[:CLASSES]
    kept_m, row_m, col_m, leaf_m, far_m = found[CLASSES:]
    over = lax.psum(over, ("leaf", "row", "col"))

    far, far_m = [lax.ppermute(v, ("leaf", "col"), both_pairs) for v in (far_move, far_m)]
    beside, beside_m = [lax.ppermute(v, "leaf", leaf_pairs) for v in (leaf_move, leaf_m)]
    near, near_m = [lax.ppermute(v, "col", col_pairs) for v in (col_move, col_m)]
    across, across_m = [lax.ppermute(v, "row", row_pairs) for v in (row_move, row_m)]
    crossed = [
        [lax.ppermute(v, "row", row_pairs) for v in pair]
        for pair in ((near, near_m), (beside, beside_m), (far, far_m))
    ]
    bufs = [kept, across, near, beside, far] + [pair[0] for pair in crossed]
    metas = [kept_m, across_m, near_m, beside_m, far_m] + [pair[1] for pair in crossed]
    owners = (0, 0, 0, 1, 1, 0, 1, 1)

    corner = panel.reshape(rows, cols, 2, ncols, tile, tile)[:, 0, :, :rows]
    corner_reg = reg.reshape(rows, cols, 2, outer, 1, tile)[:, 0, :, 0]
    inverse, upper = corner_factors(corner, corner_reg, tile)
    factor, left, right = solved_panels(
        source, where, inverse, upper, panel, (tile, nrows, ncols, rows, cols, width)
    )
    reg = reg.reshape(rows * cols * 2, outer, tile)

    def sparse():
        return merged_parent(
            source, where, metas, bufs, owners, reg, left, right,
            (tile, nrows, ncols, rows, cols, group),
        )

    def dense():
        own = untangled(flat, tile, ncols)
        other = lax.ppermute(own, "row", row_pairs)
        places = jnp.arange(ncols, dtype=i32)
        col_source = source[0][((places // rows) * cols + col_at) * rows + places % rows]
        col_index = jnp.maximum(col_source, 0)
        col_index = col_index // (rows * cols) * rows + col_index % rows
        from_next = (col_source // rows % cols != col_at)[None, :, None, None]
        col_present = (col_source >= 0)[None, :, None, None]
        halves = []
        for half in range(2):
            half_rows = half * (nrows // 2) + jnp.arange(nrows // 2, dtype=i32)
            row_source = source[0][half_rows * rows + row_at]
            row_index = jnp.maximum(row_source, 0) // rows
            is_own = (row_source % rows == row_at)[:, None, None, None]
            picked = jnp.where(
                is_own, jnp.take(own, row_index, axis=0), jnp.take(other, row_index, axis=0)
            )
            picked = jnp.where((row_source >= 0)[:, None, None, None], picked, jnp.zeros_like(picked))
            following = lax.ppermute(picked, "col", col_pairs)
            picked = jnp.where(
                from_next,
                jnp.take(following, col_index, axis=1),
                jnp.take(picked, col_index, axis=1),
            )
            picked = jnp.where(col_present, picked, jnp.zeros_like(picked))
            halves.append(picked.reshape(nrows * ncols // 2, tile, tile))
        stays = jnp.where(side == 0, halves[0], halves[1])
        leaves_here = jnp.where(side == 0, halves[1], halves[0])
        arrived = lax.ppermute(leaves_here, "leaf", leaf_pairs)
        every = nrows * ncols // 2
        codes = jnp.arange(every, dtype=i32) * rows + row_at
        codes = jnp.concatenate([jnp.full((1,), every, i32), codes])
        return merged_parent(
            source, where, [codes, codes], [stays, arrived], (0, 1), reg, left, right,
            (tile, nrows, ncols, rows, cols, group),
        )

    merged = lax.cond(over[0] > 0, dense, sparse)
    factor = factor.reshape(1, outer, cols, 1, width, tile).swapaxes(4, 5)
    merged = merged.reshape(1, outer // 2, cols, 1, tile, outer, 1, rows, tile)
    return factor, merged


def solution(mesh):
    return jax.shard_map(
        shards,
        mesh=mesh,
        in_specs=(
            P("leaf", None, None, "row", None, None, "col", None, None),
            P("leaf", None, "col", "row", None),
            P("leaf", None),
        ),
        out_specs=(
            P("leaf", None, None, "row", None, "col"),
            P("leaf", None, None, "row", None, None, "col", None, None),
        ),
        check_vma=False,
    )
```

time: 1130 us -> 409 us (0.36)
  waiting for transfers between devices: 693 us -> 138 us
  local copies, waits for them, and re-layouts: 183 us -> 5.61 us
  Pallas kernels: 0 us -> 166 us
  other arithmetic: 141 us -> 2.42 us
  matrix products: 78.8 us -> 0 us
  blocking collectives: 1.99 us -> 65.4 us
    ppermute x2 -> x16, waiting for transfers between devices: 536 us -> 138 us  [the longest x2 120 us: shards(): lax.ppermute(v, 'col', col_pairs)]
    pallas_call x0 -> x5, Pallas kernels: none -> 166 us  [the longest x1 56.3 us: corner_factors(): pl.pallas_call(functools.partial(corner_kernel, tile), out_shape=[wide, w...]
    psum x1 -> x0, waiting for transfers between devices: 107 us -> none  [broadcast(): return lax.psum(block, axis)]
    gather x4 -> x0, local copies, waits for them, and re-layouts: 73.6 us -> none  [the longest x2 39.3 us: shards(): routed = jnp.take(stacked, col_index, axis=1)]
    dot_general x1 -> x0, matrix products: 72.8 us -> none  [shards(): jnp.einsum('ik,jk->ij', all_panels, all_cols, precision=highest)]
    another operation x9 -> x4, other arithmetic: 53.7 us -> 2.2 us  [the longest x1 2.11 us: shards(): panel = lax.all_gather(jnp.stack([own_panel, sib_panel]), ('row', 'col'))]
    all_gather x2 -> x1, waiting for transfers between devices: 50.3 us -> 0.01 us  [shards(): panel = lax.all_gather(jnp.stack([own_panel, sib_panel]), ('row', 'col'))]
    psum x0 -> x1, blocking collectives: none -> 41 us  [shards(): over = lax.psum(over, ('leaf', 'row', 'col'))]
  transfers between devices with their start and end apart: 5 -> 17, of which waited for: 4 -> 6; matrix products, arithmetic and copies ran while one was open for 3% -> 1% of each run, Pallas kernels for 0% -> 31%
where the time goes in v1:
time: 409 us; the launch traced here: 407 us
  Pallas kernels  166 us (41%)
  waiting for transfers between devices  138 us (34%)
  blocking collectives  65.4 us (16%)
  starting transfers between devices  15.4 us (4%)
  between operations  14.7 us (4%)
  local copies, waits for them, and re-layouts  5.61 us (1%)
    ppermute x2, waiting for transfers between devices, shards(): lax.ppermute(v, 'col', col_pairs)  120 us
    pallas_call x1, Pallas kernels, corner_factors(): pl.pallas_call(functools.partial(corner_kernel, tile), out_shape=[wide, w...  56.3 us
    pallas_call x1, Pallas kernels, sorted_blocks(): pl.pallas_call(functools.partial(sort_kernel, dims), out_shape=[jax.Shape...  42.3 us
    psum x1, blocking collectives, shards(): over = lax.psum(over, ('leaf', 'row', 'col'))  41 us
    pallas_call x1, Pallas kernels, merged_parent(): pl.pallas_call(functools.partial(merge_kernel, dims, leaves), out_shape=j...  36.5 us
    pallas_call x1, Pallas kernels, solved_panels(): pl.pallas_call(functools.partial(solve_kernel, dims), out_shape=[jax.Shap...  28.4 us
    all_gather x1, blocking collectives, shards(): reg = lax.all_gather(gains, ('row', 'col'))  24.4 us
    ppermute x1, waiting for transfers between devices, shards(): sib_panel = lax.ppermute(own_panel, 'leaf', leaf_pairs)  12.1 us
  transfers between devices with their start and end apart: 17, of which 6 were waited for; matrix products, arithmetic and copies ran while one was open for 1% of the time, Pallas kernels for 31%

profile of v1, /device:TPU:0, one launch (start us, length us, event | category | flops | bytes accessed | tf_op | source)
XLA Modules:
  0.0 407.4 jit_solution(12475761000717852004)
XLA Ops:
  7.2 0.0 all-gather.5.cloned.1.call-start
  7.2 1.9 slice.48.x_ref
  9.1 2.2 untangle.3
  11.3 3.0 collective-permute-start.5
  14.3 12.1 %collective-permute-done.5 = bf16[16,128,128]{2,1,0:T(8,128)(2,1)S(1)} collective-permute-done((bf16[16,128,128]{2,1,0:T(8,128)(2,1)}, bf16[16,128,128]{2,1,0:T(8,128)(2,1)S(1)}, u32[]{:S(2)}, u32[]{:S(2)}) %collective-permute-start.5) | collective-permute-done | bytes 524320 | tf_op jit(solution)/shard_map/ppermute | solution.py:465
  26.4 2.1 pad_maximum_fusion
  28.6 0.0 all-gather.5.cloned.1.call-update
  28.6 1.3 concatenate.10.parent_ref
  29.8 0.1 pad_add_fusion.2.where_ref
  29.9 42.3 %sort_blocks.1 = (bf16[80,128,128]{2,1,0:T(8,128)(2,1)S(1)}, bf16[80,128,128]{2,1,0:T(8,128)(2,1)}, bf16[80,128,128]{2,1,0:T(8,128)(2,1)}, bf16[80,128,128]{2,1,...) custom-call(s32[64]{0:T(128)} %concatenate.10.parent_ref, ...), custom_call_target="tpu_custom_call" | custom-call | tf_op jit(solution)/shard_map/sort_blocks/pallas_call | solution.py:134
  72.3 3.1 collective-permute-start.14
  75.4 1.1 collective-permute-start.15
  76.5 1.0 collective-permute-start.16
  77.5 0.0 collective-permute-start.13
  77.5 117.5 %collective-permute-done.14 = bf16[80,128,128]{2,1,0:T(8,128)(2,1)} collective-permute-done((bf16[80,128,128]{2,1,0:T(8,128)(2,1)}, bf16[80,128,128]{2,1,0:T(8,128)(2,1)}, u32[]{:S(2)}, u32[]{:S(2)}) %collective-permute-start.14) | collective-permute-done | bytes 2621472 | tf_op jit(solution)/shard_map/ppermute | solution.py:482
  195.0 0.0 collective-permute-start.17
  195.0 0.0 collective-permute-done.15
  195.0 0.5 collective-permute-start.18
  195.5 0.0 collective-permute-done.16
  195.5 0.1 collective-permute-start.19
  195.6 1.6 collective-permute-start.4
  197.2 41.0 %psum.7 = s32[1]{0:T(128)} all-reduce(s32[1]{0:T(128)} %get-tuple-element.117), channel_id=1, replica_groups=mesh['leaf'=4,'row'=2,'col'=4] {'leaf','row','col'}, use_global_device_ids=true, to_apply=%region_1.2 | all-reduce | flops 1 | bytes 8 | tf_op jit(solution)/shard_map/psum | solution.py:478
  238.8 0.0 collective-permute-done.4
  238.8 0.1 collective-permute-start.6
  238.9 24.4 %all-gather.2 = f32[8,2,1024]{2,1,0:T(2,128)S(1)} all-gather(f32[1,2,1024]{2,1,0:T(2,128)S(1)} %maximum_bitcast_fusion), channel_id=3, replica_groups=mesh['leaf'=4,'row'=2,'col'=4] {'row','col'}, dimensions={0}, use_global_device_ids=true | all-gather | bytes 73728 | tf_op jit(solution)/shard_map/all_gather | solution.py:469
  263.3 0.1 reshape.352
  263.3 0.6 slice_bitcast_fusion.2.reg_ref
  263.9 0.0 collective-permute-done.6
  263.9 1.5 collective-permute-start.7
  265.4 2.2 collective-permute-done.7
  267.7 0.5 collective-permute-start.8
  268.1 0.1 copy.35
  268.3 3.0 collective-permute-done.8
  271.3 2.4 collective-permute-start.9
  273.6 0.2 fusion.19
  273.8 1.9 collective-permute-done.9
  275.8 0.1 reshape_reshape.7
  275.8 1.1 collective-permute-done.10
  276.9 0.2 collective-permute-start.11
  277.1 1.7 slice_bitcast_fusion.1.corner_ref
  278.8 56.3 %corner_factors.1 = (f32[2,256,256]{2,1,0:T(8,128)}, f32[2,256,256]{2,1,0:T(8,128)}) custom-call(bf16[2,2,2,128,128]{4,3,2,1,0:T(8,128)(2,1)} %slice_bitcast_fusion.1.corner_ref, f32[2,2,1,128]{3,2,1,0:T(1,128)} %slice_bitcast_fusion.2.reg_ref), custom_call_target="tpu_custom_call" | custom-call | tf_op jit(solution)/shard_map/corner_factors/pallas_call | solution.py:227
  335.1 0.3 collective-permute-start.12
  335.4 28.4 %solve_panels.1 = (f32[32,64,128]{2,1,0:T(8,128)}, bf16[2,16,128,768]{3,2,1,0:T(8,128)(2,1)}, bf16[2,768,2048]{2,1,0:T(8,128)(2,1)}) custom-call(s32[2,64]{1,0:T(2,128)S(1)} %broadcast_add_fusion.source_ref, s32[3]{0:T(128)S(1)} %pad_add_fusion.2.where_ref, f32[2,256,256]{2,1,0:T(8,128)} %get-tuple-element.114.inverse_ref, ...), custom_call_target="tpu_custom_call" | custom-call | tf_op jit(solution)/shard_map/solve_panels/pallas_call | solution.py:305
  363.8 0.0 collective-permute-done.12
  363.8 0.0 collective-permute-done.17
  363.8 0.0 collective-permute-done.19
  363.8 36.7 %conditional.1 = (f32[1,4,4,1,128,8,1,2,128]{8,7,6,5,4,3,2,1,0:T(2,128)}) conditional(s32[]{:T(128)} %bitcast.35, (s32[2,64]{1,0:T(2,128)S(1)}, s32[3]{0:T(128)S(1)}, s32[88]{0:T(128)S(1)}, s32[88]{0:T(128)S(1)}, s32[88]{0:T(128)S(1)}, /*index=5*/s32[88]{0:T(128)S(1)}, s32[88]{0:T(128)S(1)}, s32[88]{0:T(128)S(1)}, s32[88]{0:T(128)S(1)}, ...), branch_computations={%region_2.3_spmd, %region_3.6_spmd} | conditional | flops 75506576 | bytes 436238304 | solution.py:544
  363.8 36.5 %merge_parent.2 = f32[32768,128]{1,0:T(8,128)} custom-call(s32[2,64]{1,0:T(2,128)S(1)} %get-tuple-element.49.source_ref, s32[3]{0:T(128)S(1)} %get-tuple-element.50.where_ref, s32[88]{0:T(128)S(1)} %get-tuple-element.68.rest_0_, s32[88]{0:T(128)S(1)} %get-tuple-element.69.rest_1_, s32[88]{0:T(128)S(1)} %get-tuple-element.70.rest_2_, ...), custom_call_target="tpu_custom_call" | custom-call | tf_op jit(solution)/shard_map/cond/branch_0_fun/merge_parent/pallas_call | solution.py:405
  (17 shorter events, 0.1 us)
Async XLA Ops:
  7.2 269.9 %all-gather.5.cloned.1.call-start = ((), (), s32[]{:S(2)}) async-start(), calls=%async_computation | async-start | bytes 9437184 | tf_op jit(solution)/shard_map/all_gather | solution.py:467
  11.3 15.2 %collective-permute-start.5 = (bf16[16,128,128]{2,1,0:T(8,128)(2,1)}, bf16[16,128,128]{2,1,0:T(8,128)(2,1)S(1)}, u32[]{:S(2)}, u32[]{:S(2)}) collective-permute-start(bf16[16,128,128]{2,1,0:T(8,128)(2,1)} %bitcast.84), channel_id=1, source_target_pairs={{0,8},{8,0},{16,24},{24,16},{1,9},{9,1},{17,25},{25,17},{2,10},{10... | collective-permute-start | bytes 1572872 | tf_op jit(solution)/shard_map/ppermute | solution.py:465
  29.9 165.7 %copy-start.1 = (s32[1,62]{1,0:T(1,128)S(1)}, s32[1,62]{1,0:T(1,128)}, u32[]{:S(2)}) copy-start(s32[1,62]{1,0:T(1,128)} %param.11) | copy-start | bytes 748
  29.9 165.7 %copy-start = (f32[1,8,1,1,128]{4,3,2,1,0:T(1,128)S(1)}, f32[1,8,1,1,128]{4,3,2,1,0:T(1,128)}, u32[]{:S(2)}) copy-start(f32[1,8,1,1,128]{4,3,2,1,0:T(1,128)} %param.10) | copy-start | bytes 12292
  72.3 122.7 %collective-permute-start.14 = (bf16[80,128,128]{2,1,0:T(8,128)(2,1)}, bf16[80,128,128]{2,1,0:T(8,128)(2,1)}, u32[]{:S(2)}, u32[]{:S(2)}) collective-permute-start(bf16[80,128,128]{2,1,0:T(8,128)(2,1)} %get-tuple-element.125), channel_id=1, source_target_pairs={{0,3},{1,0},{2,1},{3,2},{4,7},{5,4},{6,5},{7,6},{8,11},{9,8},{10,9... | collective-permute-start | bytes 7864328 | tf_op jit(solution)/shard_map/ppermute | solution.py:482
  75.4 119.6 %collective-permute-start.15 = (bf16[80,128,128]{2,1,0:T(8,128)(2,1)}, bf16[80,128,128]{2,1,0:T(8,128)(2,1)}, u32[]{:S(2)}, u32[]{:S(2)}) collective-permute-start(bf16[80,128,128]{2,1,0:T(8,128)(2,1)} %get-tuple-element.126), channel_id=1, source_target_pairs={{0,8},{8,0},{16,24},{24,16},{1,9},{9,1},{17,25},{25,17},{2,10},{10... | collective-permute-start | bytes 7864328 | tf_op jit(solution)/shard_map/ppermute | solution.py:481
  76.5 119.0 %collective-permute-start.16 = (bf16[80,128,128]{2,1,0:T(8,128)(2,1)}, bf16[80,128,128]{2,1,0:T(8,128)(2,1)}, u32[]{:S(2)}, u32[]{:S(2)}) collective-permute-start(bf16[80,128,128]{2,1,0:T(8,128)(2,1)} %get-tuple-element.127), channel_id=1, source_target_pairs={{0,11},{1,8},{2,9},{3,10},{8,3},{9,0},{10,1},{11,2},{16,27},{17,24... | collective-permute-start | bytes 7864328 | tf_op jit(solution)/shard_map/ppermute | solution.py:480
  77.5 286.3 %collective-permute-start.13 = (bf16[80,128,128]{2,1,0:T(8,128)(2,1)}, bf16[80,128,128]{2,1,0:T(8,128)(2,1)}, u32[]{:S(2)}, u32[]{:S(2)}) collective-permute-start(bf16[80,128,128]{2,1,0:T(8,128)(2,1)} %get-tuple-element.124), channel_id=1, source_target_pairs={{0,4},{4,0},{1,5},{5,1},{2,6},{6,2},{3,7},{7,3},{8,12},{12,8},{9,1... | collective-permute-start | bytes 7864328 | tf_op jit(solution)/shard_map/ppermute | solution.py:483
  195.0 168.8 %collective-permute-start.17 = (bf16[80,128,128]{2,1,0:T(8,128)(2,1)}, bf16[80,128,128]{2,1,0:T(8,128)(2,1)}, u32[]{:S(2)}, u32[]{:S(2)}) collective-permute-start(bf16[80,128,128]{2,1,0:T(8,128)(2,1)} %collective-permute-done.14), channel_id=1, source_target_pairs={{0,4},{4,0},{1,5},{5,1},{2,6},{6,2},{3,7},{7,3},{8,12},{12,8},{9,1... | collective-permute-start | bytes 7864328 | tf_op jit(solution)/shard_map/ppermute | solution.py:485
  195.0 168.8 %collective-permute-start.18 = (bf16[80,128,128]{2,1,0:T(8,128)(2,1)}, bf16[80,128,128]{2,1,0:T(8,128)(2,1)}, u32[]{:S(2)}, u32[]{:S(2)}) collective-permute-start(bf16[80,128,128]{2,1,0:T(8,128)(2,1)} %collective-permute-done.15), channel_id=1, source_target_pairs={{0,4},{4,0},{1,5},{5,1},{2,6},{6,2},{3,7},{7,3},{8,12},{12,8},{9,1... | collective-permute-start | bytes 7864328 | tf_op jit(solution)/shard_map/ppermute | solution.py:485
  195.5 168.3 %collective-permute-start.19 = (bf16[80,128,128]{2,1,0:T(8,128)(2,1)}, bf16[80,128,128]{2,1,0:T(8,128)(2,1)}, u32[]{:S(2)}, u32[]{:S(2)}) collective-permute-start(bf16[80,128,128]{2,1,0:T(8,128)(2,1)} %collective-permute-done.16), channel_id=1, source_target_pairs={{0,4},{4,0},{1,5},{5,1},{2,6},{6,2},{3,7},{7,3},{8,12},{12,8},{9,1... | collective-permute-start | bytes 7864328 | tf_op jit(solution)/shard_map/ppermute | solution.py:485
  195.6 43.2 %collective-permute-start.4 = (f32[1086]{0:T(1024)S(1)}, f32[1086]{0:T(1024)S(1)}, u32[]{:S(2)}, u32[]{:S(2)}) collective-permute-start(f32[1086]{0:T(1024)S(1)} %pad_maximum_fusion.1), channel_id=1, source_target_pairs={{0,8},{8,0},{16,24},{24,16},{1,9},{9,1},{17,25},{25,17},{2,10},{10... | collective-permute-start | bytes 13040 | tf_op jit(solution)/shard_map/ppermute | solution.py:466
  238.8 25.1 %collective-permute-start.6 = (s32[88]{0:T(128)}, s32[88]{0:T(128)S(1)}, u32[]{:S(2)}, u32[]{:S(2)}) collective-permute-start(s32[88]{0:T(128)} %get-tuple-element.119), channel_id=1, source_target_pairs={{0,4},{4,0},{1,5},{5,1},{2,6},{6,2},{3,7},{7,3},{8,12},{12,8},{9,1... | collective-permute-start | bytes 1064 | tf_op jit(solution)/shard_map/ppermute | solution.py:483
  263.9 3.8 collective-permute-start.7
  267.7 3.6 collective-permute-start.8
  271.3 4.5 %collective-permute-start.9 = (s32[88]{0:T(128)}, s32[88]{0:T(128)S(1)}, u32[]{:S(2)}, u32[]{:S(2)}) collective-permute-start(s32[88]{0:T(128)} %get-tuple-element.122), channel_id=1, source_target_pairs={{0,11},{1,8},{2,9},{3,10},{8,3},{9,0},{10,1},{11,2},{16,27},{17,24... | collective-permute-start | bytes 1064 | tf_op jit(solution)/shard_map/ppermute | solution.py:480
  275.8 1.1 collective-permute-start.10
  276.9 58.2 %collective-permute-start.11 = (s32[88]{0:T(128)S(1)}, s32[88]{0:T(128)S(1)}, u32[]{:S(2)}, u32[]{:S(2)}) collective-permute-start(s32[88]{0:T(128)S(1)} %collective-permute-done.8), channel_id=1, source_target_pairs={{0,4},{4,0},{1,5},{5,1},{2,6},{6,2},{3,7},{7,3},{8,12},{12,8},{9,1... | collective-permute-start | bytes 1064 | tf_op jit(solution)/shard_map/ppermute | solution.py:485
  335.1 28.7 %collective-permute-start.12 = (s32[88]{0:T(128)S(1)}, s32[88]{0:T(128)S(1)}, u32[]{:S(2)}, u32[]{:S(2)}) collective-permute-start(s32[88]{0:T(128)S(1)} %collective-permute-done.9), channel_id=1, source_target_pairs={{0,4},{4,0},{1,5},{5,1},{2,6},{6,2},{3,7},{7,3},{8,12},{12,8},{9,1... | collective-permute-start | bytes 1064 | tf_op jit(solution)/shard_map/ppermute | solution.py:485
Sparse Core Ops, SparseCore 0:
  28.7 63.0 all-gather.4

commit v2 on v1

--- a/solution.py
+++ b/solution.py
@@ -35,123 +35,181 @@
     )(x)
 
 
-def sort_kernel(dims, parent_ref, where_ref, x_ref, *rest):
-    tile, nrows, ncols, rows, cols, cap = dims
-    bufs = rest[:CLASSES]
-    metas = rest[CLASSES : 2 * CLASSES]
-    over_ref = rest[2 * CLASSES]
-    wide, blocks, seen, found_v, found, counts, sem, found_sem = rest[2 * CLASSES + 1 :]
-    step = pl.program_id(0)
+def panel_kernel(tile, ncols, outer, x_ref, reg_ref, out_ref, wide):
     wide[...] = x_ref[...].astype(f32)
     for j in range(ncols):
-        block = wide[pl.ds(j, tile, stride=ncols), :]
-        at = step * ncols + j
-        blocks[at] = block.astype(bf16)
-        top = jnp.max(jnp.abs(block), axis=0, keepdims=True)
-        seen[pl.ds(at, 1), :] = jnp.where(top > 0, 1.0, 0.0)
-
-    @pl.when(step == nrows - 1)
+        out_ref[pl.ds(j * tile, tile)] = wide[pl.ds(j, tile, stride=ncols), :].astype(bf16)
+    pieces = [piece.astype(f32) for piece in split3(reg_ref[...])]
+    pad = out_ref.shape[0] - ncols * tile - 3 * outer
+    tail = jnp.concatenate(pieces + [jnp.zeros((pad, tile), f32)], axis=0)
+    out_ref[pl.ds(ncols * tile, 3 * outer + pad)] = tail.astype(bf16)
+
+
+def panel_and_gains(x, reg, tile, ncols):
+    outer = reg.shape[0]
+    tail = -(-(3 * outer + 1) // 16) * 16
+    return pl.pallas_call(
+        functools.partial(panel_kernel, tile, ncols, outer),
+        out_shape=jax.ShapeDtypeStruct((ncols * tile + tail, tile), bf16),
+        scratch_shapes=[pltpu.VMEM((tile * ncols, tile), f32)],
+        grid=(1,),
+        in_specs=[
+            pl.BlockSpec((tile * ncols, tile), lambda i: (0, 0)),
+            pl.BlockSpec((outer, tile), lambda i: (0, 0)),
+        ],
+        out_specs=pl.BlockSpec((ncols * tile + tail, tile), lambda i: (0, 0)),
+        name="panel_and_gains",
+    )(x, reg)
+
+
+def flag_kernel(tile, ncols, x_ref, hits_ref, seen):
+    step = pl.program_id(0)
+    lines = tile * ncols
+    group = x_ref.shape[0] // lines
+    for g in range(group):
+        x = x_ref[g * lines : (g + 1) * lines]
+        at = pl.multiple_of((step * group + g) * ncols, ncols)
+        if ncols % 16 == 0:
+            top = jnp.max(jnp.abs(x).reshape(tile, ncols, tile), axis=0)
+            seen[pl.ds(at, ncols)] = top.astype(f32)
+        else:
+            top = jnp.max(jnp.abs(x.astype(f32)).reshape(tile, ncols, tile), axis=0)
+            for j in range(ncols):
+                seen[pl.ds(at + j, 1)] = top[j : j + 1]
+
+    @pl.when(step == pl.num_programs(0) - 1)
     def _():
-        hits = lax.dot_general(
+        hits_ref[...] = lax.dot_general(
             jnp.ones((8, tile), f32),
-            seen[...],
+            jnp.where(seen[...] > 0, 1.0, 0.0),
             (((1,), (1,)), ((), ())),
             preferred_element_type=f32,
         )
-        found_v[...] = hits.astype(i32)
-        copy = pltpu.make_async_copy(found_v, found, found_sem)
-        copy.start()
-        side = where_ref[0]
-        row_at = where_ref[1]
-        col_at = where_ref[2]
-        half = nrows * rows // 2
+
+
+def block_flags(x, tile, nrows, ncols):
+    count = nrows * ncols
+    return pl.pallas_call(
+        functools.partial(flag_kernel, tile, ncols),
+        out_shape=jax.ShapeDtypeStruct((8, count), f32),
+        grid=(nrows // 4,),
+        in_specs=[pl.BlockSpec((4 * tile * ncols, tile), lambda i: (i, 0))],
+        out_specs=pl.BlockSpec((8, count), lambda i: (0, 0)),
+        scratch_shapes=[pltpu.VMEM((count, tile), f32)],
+        compiler_params=pltpu.CompilerParams(vmem_limit_bytes=VMEM_LIMIT),
+        cost_estimate=pl.CostEstimate(flops=0, bytes_accessed=30_000_000, transcendentals=0),
+        name="block_flags",
+    )(x)
+
+
+def sort_kernel(dims, entry_ref, x_ref, *rest):
+    tile, group, ncols, cap = dims
+    bufs = rest[:CLASSES]
+    wide, blocks, lists, lists_low, counts, sem = rest[CLASSES:]
+    step = pl.program_id(0)
+    lines = tile * ncols
+    lane = lax.broadcasted_iota(i32, (8, tile), 1)
+    sublane = lax.broadcasted_iota(i32, (8, tile), 0)
+
+    @pl.when(step == 0)
+    def _():
+        lists[...] = jnp.zeros_like(lists)
         for k in range(CLASSES):
             counts[k] = 0
-        copy.wait()
-
-        def one_row(i, carry):
-            parent_row = parent_ref[i * rows + row_at]
-
-            @pl.when(parent_row >= 0)
+
+    for g in range(group):
+        wide[g] = x_ref[g * lines : (g + 1) * lines].astype(f32)
+
+    def one_row(g, carry):
+        for j in range(ncols):
+            at = (step * group + g) * ncols + j
+            entry = entry_ref[at]
+
+            @pl.when(entry >= 0)
             def _():
-                moves_leaf = parent_row // half != side
-                target_row = parent_row % rows
-                moves_row = target_row != row_at
-                place_row = parent_row // rows % (nrows // 2)
-
-                def one_col(j, inner):
-                    source_col = ((j // rows) * cols + col_at) * rows + j % rows
-                    parent_col = parent_ref[source_col]
-
-                    @pl.when((found[0, i * ncols + j] > 0) & (parent_col >= 0))
+                kind = entry % 8
+                code = entry // 8
+                slot = counts[kind]
+                counts[kind] = slot + 1
+                blocks[at] = wide[g, pl.ds(j, tile, stride=ncols), :].astype(bf16)
+                here = jnp.where(sublane == 0, code // 256, code % 256).astype(f32)
+                lists[kind] = jnp.where(lane == slot, here, lists[kind])
+                for k in range(CLASSES):
+
+                    @pl.when((kind == k) & (slot < cap))
                     def _():
-                        moves_col = parent_col // rows % cols != col_at
-                        place_col = parent_col // (rows * cols) * rows + parent_col % rows
-                        kind = jnp.where(
-                            moves_leaf,
-                            jnp.where(moves_col, 4, 3),
-                            jnp.where(moves_col, 2, jnp.where(moves_row, 1, 0)),
-                        )
-                        slot = counts[kind]
-                        counts[kind] = slot + 1
-                        code = (place_row * ncols + place_col) * rows + target_row
-                        for k in range(CLASSES):
-
-                            @pl.when((kind == k) & (slot < cap))
-                            def _():
-                                metas[k][1 + slot] = code
-                                pltpu.make_async_copy(
-                                    blocks.at[i * ncols + j], bufs[k].at[slot], sem
-                                ).start()
-
-                    return inner
-
-                lax.fori_loop(0, ncols, one_col, 0)
-
-            return carry
-
-        lax.fori_loop(0, nrows, one_row, 0)
+                        pltpu.make_async_copy(blocks.at[at], bufs[k].at[slot], sem).start()
+
+        return carry
+
+    lax.fori_loop(0, group, one_row, 0)
+
+    @pl.when(step == pl.num_programs(0) - 1)
+    def _():
         sent = 0
-        over = 0
         for k in range(CLASSES):
             taken = jnp.minimum(counts[k], cap)
-            metas[k][0] = taken
             sent = sent + taken
-            over = over + (counts[k] - taken)
-        over_ref[0] = over
+            listed = jnp.where(sublane == 2, taken.astype(f32), lists[k])
+            lists_low[k] = jnp.concatenate([listed, listed], axis=0).astype(bf16)
+        copies = [
+            pltpu.make_async_copy(lists_low.at[k], bufs[k].at[cap, pl.ds(0, 16)], sem)
+            for k in range(CLASSES)
+        ]
+        for copy in copies:
+            copy.start()
 
         def drain(_, carry):
             pltpu.make_async_copy(blocks.at[0], bufs[0].at[0], sem).wait()
             return carry
 
         lax.fori_loop(0, sent, drain, 0)
-
-
-def sorted_blocks(x, parent, where, dims):
-    tile, nrows, ncols, rows, cols, cap = dims
-    count = nrows * ncols
+        for copy in copies:
+            copy.wait()
+
+
+def sorted_blocks(x, entries, dims):
+    tile, nrows, ncols, cap = dims
+    group = 4
     smem = pl.BlockSpec(memory_space=pltpu.SMEM)
     return pl.pallas_call(
-        functools.partial(sort_kernel, dims),
-        out_shape=[jax.ShapeDtypeStruct((cap, tile, tile), bf16)] * CLASSES
-        + [jax.ShapeDtypeStruct((cap + 8,), i32)] * CLASSES
-        + [jax.ShapeDtypeStruct((1,), i32)],
-        grid=(nrows,),
-        in_specs=[smem, smem, pl.BlockSpec((tile * ncols, tile), lambda i: (i, 0))],
-        out_specs=[pl.BlockSpec(memory_space=pl.ANY)] * CLASSES + [smem] * (CLASSES + 1),
+        functools.partial(sort_kernel, (tile, group, ncols, cap)),
+        out_shape=[jax.ShapeDtypeStruct((cap + 1, tile, tile), bf16)] * CLASSES,
+        grid=(nrows // group,),
+        in_specs=[smem, pl.BlockSpec((group * tile * ncols, tile), lambda i: (i, 0))],
+        out_specs=[pl.BlockSpec(memory_space=pl.ANY)] * CLASSES,
         scratch_shapes=[
-            pltpu.VMEM((tile * ncols, tile), f32),
-            pltpu.VMEM((count, tile, tile), bf16),
-            pltpu.VMEM((count, tile), f32),
-            pltpu.VMEM((8, count), i32),
-            pltpu.SMEM((8, count), i32),
+            pltpu.VMEM((group, tile * ncols, tile), f32),
+            pltpu.VMEM((nrows * ncols, tile, tile), bf16),
+            pltpu.VMEM((CLASSES, 8, tile), f32),
+            pltpu.VMEM((CLASSES, 16, tile), bf16),
             pltpu.SMEM((CLASSES,), i32),
-            pltpu.SemaphoreType.DMA,
             pltpu.SemaphoreType.DMA,
         ],
         compiler_params=pltpu.CompilerParams(vmem_limit_bytes=VMEM_LIMIT),
+        cost_estimate=pl.CostEstimate(flops=0, bytes_accessed=60_000_000, transcendentals=0),
         name="sort_blocks",
-    )(parent, where, x)
+    )(entries, x)
+
+
+def block_moves(own_map, side, row_at, col_at, nrows, ncols, rows, cols):
+    parent = jnp.concatenate([jnp.full((NPAN * rows,), -1, i32), own_map])
+    at_row = parent.reshape(nrows, rows)
+    at_row = jnp.where(row_at == 0, at_row[:, 0], at_row[:, 1])[:, None]
+    at_col = parent.reshape(nrows // cols, cols, rows)
+    at_col = lax.dynamic_index_in_dim(at_col, col_at, 1, keepdims=False).reshape(1, ncols)
+    moves_leaf = at_row // (nrows * rows // 2) != side
+    moves_col = at_col // rows % cols != col_at
+    moves_row = at_row % rows != row_at
+    kind = jnp.where(
+        moves_leaf,
+        jnp.where(moves_col, 4, 3),
+        jnp.where(moves_col, 2, jnp.where(moves_row, 1, 0)),
+    )
+    place_row = at_row // rows % (nrows // 2)
+    place_col = at_col // (rows * cols) * rows + at_col % rows
+    code = (place_row * ncols + place_col) * rows + at_row % rows
+    return jnp.where((at_row >= 0) & (at_col >= 0), code * 8 + kind, -1).reshape(-1)
 
 
 def eliminate(work, tile):
@@ -178,15 +236,38 @@
     return jnp.dot(a, b, precision=HIGHEST, preferred_element_type=f32)
 
 
-def corner_kernel(tile, corner_ref, reg_ref, inverse_ref, upper_ref, work):
+def corner_kernel(
+    dims, where_ref, mine_ref, other_ref, inverse_ref, upper_ref, work, tiles, tails, sem
+):
+    tile, ncols, outer, cols = dims
+    row_at = where_ref[1]
+    first = lax.rem(cols - where_ref[2], cols)
+    tail = tails.shape[2]
+    copies = []
+    for which, ref in ((0, mine_ref), (1, other_ref)):
+        at = row_at if which == 0 else 1 - row_at
+        copies.append(
+            pltpu.make_async_copy(ref.at[first, :, pl.ds(0, 2 * tile)], tiles.at[at], sem.at[0, which])
+        )
+        copies.append(
+            pltpu.make_async_copy(
+                ref.at[first, :, pl.ds(ncols * tile, tail)], tails.at[at], sem.at[1, which]
+            )
+        )
+    for copy in copies:
+        copy.start()
+    for copy in copies:
+        copy.wait()
     rows = lax.broadcasted_iota(i32, (tile, tile), 0)
     lanes = lax.broadcasted_iota(i32, (tile, tile), 1)
     eye = jnp.where(rows == lanes, 1.0, 0.0).astype(f32)
 
     def block(leaf, i, j):
-        value = corner_ref[i, leaf, j].astype(f32)
+        value = tiles[i, leaf, j * tile : (j + 1) * tile, :].astype(f32)
         if i == j:
-            value = value + jnp.where(rows == lanes, reg_ref[i, leaf], 0.0)
+            pieces = tails[i, leaf].astype(f32)
+            gain = pieces[:1] + pieces[outer : outer + 1] + pieces[2 * outer : 2 * outer + 1]
+            value = value + jnp.where(rows == lanes, gain, 0.0)
         return value
 
     def finish(leaf):
@@ -222,14 +303,25 @@
         inverse_ref[leaf, tile:, :tile] = -full_dot(inverse, low)
 
 
-def corner_factors(corner, reg, tile):
+def corner_factors(where, mine, other, tile, ncols, outer):
     wide = jax.ShapeDtypeStruct((2, 2 * tile, 2 * tile), f32)
+    tail = mine.shape[2] - ncols * tile
+    hbm = pl.BlockSpec(memory_space=pl.ANY)
+    vmem = pl.BlockSpec(memory_space=pltpu.VMEM)
     return pl.pallas_call(
-        functools.partial(corner_kernel, tile),
+        functools.partial(corner_kernel, (tile, ncols, outer, mine.shape[0])),
         out_shape=[wide, wide],
-        scratch_shapes=[pltpu.VMEM((2, tile, 2 * tile), f32)],
+        in_specs=[pl.BlockSpec(memory_space=pltpu.SMEM), hbm, hbm],
+        out_specs=[vmem, vmem],
+        scratch_shapes=[
+            pltpu.VMEM((2, tile, 2 * tile), f32),
+            pltpu.VMEM((2, 2, 2 * tile, tile), bf16),
+            pltpu.VMEM((2, 2, tail, tile), bf16),
+            pltpu.SemaphoreType.DMA((2, 2)),
+        ],
+        cost_estimate=pl.CostEstimate(flops=0, bytes_accessed=200_000_000, transcendentals=0),
         name="corner_factors",
-    )(corner, reg)
+    )(where, mine, other)
 
 
 def split3(x):
@@ -240,10 +332,28 @@
     return high, mid, low
 
 
-def solve_kernel(dims, source_ref, where_ref, inverse_ref, upper_ref, panel_ref, *rest):
+def solve_kernel(dims, source_ref, where_ref, inverse_ref, upper_ref, mine_ref, other_ref, *rest):
     tile, nrows, ncols, rows, cols, width = dims
-    factor_ref, left_ref, right_ref = rest
+    factor_ref, left_ref, right_ref, gains_ref, panel, sem = rest
     row_at = where_ref[1]
+    col_at = where_ref[2]
+    outer = ncols // rows
+    copies = [
+        pltpu.make_async_copy(ref.at[k], panel.at[place, lax.rem(col_at + k, cols)], sem)
+        for ref, place in ((mine_ref, row_at), (other_ref, 1 - row_at))
+        for k in range(cols)
+    ]
+    for copy in copies:
+        copy.start()
+    for copy in copies:
+        copy.wait()
+    for s in range(rows):
+        for c in range(cols):
+            for leaf in range(2):
+                pieces = panel[s, c, leaf, ncols * tile :, :].astype(f32)
+                gains_ref[(s * cols + c) * 2 + leaf] = (
+                    pieces[:outer] + pieces[outer : 2 * outer] + pieces[2 * outer : 3 * outer]
+                )
     col_at = where_ref[2]
     half = nrows * rows // 2
     side = where_ref[0]
@@ -251,7 +361,8 @@
     def raw(leaf, block):
         at = block // rows % cols
         j = block // (rows * cols) * rows + block % rows
-        return jnp.concatenate([panel_ref[s * cols + at, leaf, j] for s in range(rows)], axis=0)
+        lines = pl.ds(pl.multiple_of(j * tile, tile), tile)
+        return jnp.concatenate([panel[s, at, leaf, lines, :] for s in range(rows)], axis=0)
 
     def dots(pieces, value):
         total = jnp.dot(pieces[0], value, preferred_element_type=f32)
@@ -297,10 +408,11 @@
         lax.fori_loop(0, nrows // 2, left, 0)
 
 
-def solved_panels(source, where, inverse, upper, panel, dims):
+def solved_panels(source, where, inverse, upper, mine, other, dims):
     tile, nrows, ncols, rows, cols, width = dims
     smem = pl.BlockSpec(memory_space=pltpu.SMEM)
     vmem = pl.BlockSpec(memory_space=pltpu.VMEM)
+    hbm = pl.BlockSpec(memory_space=pl.ANY)
     depth = 3 * rows * tile
     return pl.pallas_call(
         functools.partial(solve_kernel, dims),
@@ -308,21 +420,26 @@
             jax.ShapeDtypeStruct((nrows, width, tile), f32),
             jax.ShapeDtypeStruct((2, nrows // 2, tile, depth), bf16),
             jax.ShapeDtypeStruct((2, depth, ncols * tile), bf16),
+            jax.ShapeDtypeStruct((rows * cols * 2, ncols // rows, tile), f32),
         ],
-        in_specs=[smem, smem, vmem, vmem, vmem],
-        out_specs=[vmem, vmem, vmem],
+        in_specs=[smem, smem, vmem, vmem, hbm, hbm],
+        out_specs=[vmem] * 4,
+        scratch_shapes=[
+            pltpu.VMEM((rows,) + mine.shape, bf16),
+            pltpu.SemaphoreType.DMA,
+        ],
         compiler_params=pltpu.CompilerParams(vmem_limit_bytes=VMEM_LIMIT),
+        cost_estimate=pl.CostEstimate(flops=0, bytes_accessed=100_000_000, transcendentals=0),
         name="solve_panels",
-    )(source, where, inverse, upper, panel)
+    )(source, where, inverse, upper, mine, other)
 
 
 def merge_kernel(dims, leaves, source_ref, where_ref, *rest):
     tile, nrows, ncols, rows, cols, group = dims
     count = len(leaves)
-    metas = rest[:count]
-    bufs = rest[count : 2 * count]
-    reg_ref, left_ref, right_ref, out_ref = rest[2 * count : 2 * count + 4]
-    table, blocks, totals, sem = rest[2 * count + 4 :]
+    bufs = rest[:count]
+    reg_ref, left_ref, right_ref, out_ref = rest[count : count + 4]
+    table, blocks, totals, lists_low, lists_v, lists, sem = rest[count + 4 :]
     step = pl.program_id(0)
     side = where_ref[0]
     row_at = where_ref[1]
@@ -336,13 +453,30 @@
             table[i] = 0
             return carry
 
+        copies = [
+            pltpu.make_async_copy(
+                bufs[k].at[bufs[k].shape[0] - 1, pl.ds(0, 16)], lists_low.at[k], sem
+            )
+            for k in range(count)
+        ]
+        for copy in copies:
+            copy.start()
         lax.fori_loop(0, 2 * per_leaf, clear, 0)
         blocks[0] = jnp.zeros((tile, tile), bf16)
         filled = 1
+        for copy in copies:
+            copy.wait()
         for k in range(count):
+            listed = lists_low[k].astype(f32)
+            codes = listed[0:1] * 256.0 + listed[1:2]
+            lists_v[k] = jnp.concatenate([codes, listed[2:3]] + [codes] * 6, axis=0).astype(i32)
+        copy = pltpu.make_async_copy(lists_v, lists, sem)
+        copy.start()
+        copy.wait()
+        for k in range(count):
 
             def place(e, slot):
-                code = metas[k][1 + e]
+                code = lists[k, 0, e]
                 mine = code % rows == row_at
 
                 @pl.when(mine)
@@ -352,7 +486,7 @@
 
                 return slot + jnp.where(mine, 1, 0)
 
-            filled = lax.fori_loop(0, metas[k][0], place, filled)
+            filled = lax.fori_loop(0, lists[k, 1, 0], place, filled)
 
         def drain(_, carry):
             pltpu.make_async_copy(bufs[0].at[0], blocks.at[0], sem).wait()
@@ -395,7 +529,7 @@
             out_ref[pl.ds(g * tile * ncols + j, tile, stride=ncols), :] = parts[0] + parts[1]
 
 
-def merged_parent(source, where, metas, bufs, leaves, reg, left, right, dims):
+def merged_parent(source, where, bufs, leaves, reg, left, right, dims):
     tile, nrows, ncols, rows, cols, group = dims
     count = len(leaves)
     smem = pl.BlockSpec(memory_space=pltpu.SMEM)
@@ -406,7 +540,7 @@
         functools.partial(merge_kernel, dims, leaves),
         out_shape=jax.ShapeDtypeStruct((nrows // 2 * tile * ncols, tile), f32),
         grid=(nrows // 2 // group,),
-        in_specs=[smem] * (2 + count)
+        in_specs=[smem] * 2
         + [hbm] * count
         + [
             vmem,
@@ -418,11 +552,14 @@
             pltpu.SMEM((nrows * ncols,), i32),
             pltpu.VMEM((nrows * ncols + 1, tile, tile), bf16),
             pltpu.VMEM((2, group * tile, ncols * tile), f32),
+            pltpu.VMEM((count, 16, tile), bf16),
+            pltpu.VMEM((count, 8, tile), i32),
+            pltpu.SMEM((count, 8, tile), i32),
             pltpu.SemaphoreType.DMA,
         ],
         compiler_params=pltpu.CompilerParams(vmem_limit_bytes=VMEM_LIMIT),
         name="merge_parent",
-    )(source, where, *metas, *bufs, reg, left, right)
+    )(source, where, *bufs, reg, left, right)
 
 
 def sparse_sources(child_map, blocks, panel_blocks):
@@ -458,48 +595,57 @@
         for j in range(cols)
     ]
 
-    own_panel = untangled(flat[: tile * ncols], tile, ncols)[0]
-    own_small = jnp.concatenate(
-        [regular.reshape(-1), child_map.reshape(-1).astype(f32)]
+    def from_each_col(value):
+        pairs = [[(j, (j - k) % cols) for j in range(cols)] for k in range(cols)]
+        return [value] + [lax.ppermute(value, "col", pairs[k]) for k in range(1, cols)]
+
+    own_panel = panel_and_gains(flat, regular.reshape(outer, tile), tile, ncols)
+    own_map = child_map.reshape(-1)
+    sib_panel = lax.ppermute(own_panel, "leaf", leaf_pairs)
+    sib_map = lax.ppermute(own_map, "leaf", leaf_pairs)
+    own_panels = from_each_col(own_panel)
+    maps = jnp.stack([own_map, sib_map])
+    source = sparse_sources(maps, blocks, NPAN * rows)
+
+    hits = block_flags(flat, tile, nrows, ncols)
+    moves = block_moves(own_map, side, row_at, col_at, nrows, ncols, rows, cols)
+    entries = jnp.where(hits[0] > 0, moves, -1)
+    kinds = jnp.arange(CLASSES, dtype=i32)[:, None]
+    counts = jnp.sum(((entries >= 0)[None, :] & (entries % 8 == kinds)).astype(i32), axis=1)
+    over = jnp.max(counts, keepdims=True) - cap
+    sib_panel, entries, over = lax.optimization_barrier((sib_panel, entries, over))
+    over = jnp.maximum(over, lax.ppermute(over, "leaf", leaf_pairs))
+    mark = jnp.where(over > 0, 1.0, 0.0).astype(bf16)
+    mark_row = own_panel.shape[0] - 1
+    sib_panel = lax.dynamic_update_slice(
+        sib_panel, jnp.broadcast_to(mark[:, None], (1, tile)), (mark_row, 0)
     )
-    sib_panel = lax.ppermute(own_panel, "leaf", leaf_pairs)
-    sib_small = lax.ppermute(own_small, "leaf", leaf_pairs)
-    panel = lax.all_gather(jnp.stack([own_panel, sib_panel]), ("row", "col"))
-    gains = jnp.stack([own_small[: outer * tile], sib_small[: outer * tile]])
-    reg = lax.all_gather(gains, ("row", "col"))
-    reg = reg.reshape(rows * cols, 2, outer, tile)
-    maps = jnp.stack([child_map.reshape(-1), sib_small[outer * tile :].astype(i32)])
-    source = sparse_sources(maps, blocks, NPAN * rows)
-
-    parent = jnp.concatenate([jnp.full((NPAN * rows,), -1, i32), child_map.reshape(-1)])
-    *found, over = sorted_blocks(flat, parent, where, (tile, nrows, ncols, rows, cols, cap))
-    kept, row_move, col_move, leaf_move, far_move = found[:CLASSES]
-    kept_m, row_m, col_m, leaf_m, far_m = found[CLASSES:]
-    over = lax.psum(over, ("leaf", "row", "col"))
-
-    far, far_m = [lax.ppermute(v, ("leaf", "col"), both_pairs) for v in (far_move, far_m)]
-    beside, beside_m = [lax.ppermute(v, "leaf", leaf_pairs) for v in (leaf_move, leaf_m)]
-    near, near_m = [lax.ppermute(v, "col", col_pairs) for v in (col_move, col_m)]
-    across, across_m = [lax.ppermute(v, "row", row_pairs) for v in (row_move, row_m)]
-    crossed = [
-        [lax.ppermute(v, "row", row_pairs) for v in pair]
-        for pair in ((near, near_m), (beside, beside_m), (far, far_m))
-    ]
-    bufs = [kept, across, near, beside, far] + [pair[0] for pair in crossed]
-    metas = [kept_m, across_m, near_m, beside_m, far_m] + [pair[1] for pair in crossed]
+    sib_panels = from_each_col(sib_panel)
+    found = sorted_blocks(flat, entries, (tile, nrows, ncols, cap))
+    found, own_panels, sib_panels, source = lax.optimization_barrier(
+        (found, own_panels, sib_panels, source)
+    )
+    kept, row_move, col_move, leaf_move, far_move = found
+    far = lax.ppermute(far_move, ("leaf", "col"), both_pairs)
+    beside = lax.ppermute(leaf_move, "leaf", leaf_pairs)
+    near = lax.ppermute(col_move, "col", col_pairs)
+    across = lax.ppermute(row_move, "row", row_pairs)
+    mine = jnp.stack([jnp.stack(pair) for pair in zip(own_panels, sib_panels)])
+    other = lax.ppermute(mine, "row", row_pairs)
+    inverse, upper = corner_factors(where, mine, other, tile, ncols, outer)
+    factor, left, right, reg = solved_panels(
+        source, where, inverse, upper, mine, other, (tile, nrows, ncols, rows, cols, width)
+    )
+    marks = jnp.concatenate([mine[:, 1, mark_row, 0], other[:, 1, mark_row, 0]])
+    over = jnp.max(marks.astype(f32)) > 0
+    near, beside, far, left, right = lax.optimization_barrier((near, beside, far, left, right))
+    crossed = [lax.ppermute(v, "row", row_pairs) for v in (near, beside, far)]
+    bufs = [kept, across, near, beside, far] + crossed
     owners = (0, 0, 0, 1, 1, 0, 1, 1)
-
-    corner = panel.reshape(rows, cols, 2, ncols, tile, tile)[:, 0, :, :rows]
-    corner_reg = reg.reshape(rows, cols, 2, outer, 1, tile)[:, 0, :, 0]
-    inverse, upper = corner_factors(corner, corner_reg, tile)
-    factor, left, right = solved_panels(
-        source, where, inverse, upper, panel, (tile, nrows, ncols, rows, cols, width)
-    )
-    reg = reg.reshape(rows * cols * 2, outer, tile)
 
     def sparse():
         return merged_parent(
-            source, where, metas, bufs, owners, reg, left, right,
+            source, where, bufs, owners, reg, left, right,
             (tile, nrows, ncols, rows, cols, group),
         )
 
@@ -534,14 +680,21 @@
         leaves_here = jnp.where(side == 0, halves[1], halves[0])
         arrived = lax.ppermute(leaves_here, "leaf", leaf_pairs)
         every = nrows * ncols // 2
-        codes = jnp.arange(every, dtype=i32) * rows + row_at
-        codes = jnp.concatenate([jnp.full((1,), every, i32), codes])
+        part = min(every, tile)
+        bufs = []
+        for value in (stays, arrived):
+            for first in range(0, every, part):
+                codes = (first + jnp.arange(tile, dtype=i32)) * rows + row_at
+                listed = jnp.stack([codes // 256, codes % 256, jnp.full((tile,), part, i32)])
+                listed = jnp.pad(listed, ((0, tile - 3), (0, 0))).astype(bf16)
+                bufs.append(jnp.concatenate([value[first : first + part], listed[None]]))
+        owners = (0,) * (len(bufs) // 2) + (1,) * (len(bufs) // 2)
         return merged_parent(
-            source, where, [codes, codes], [stays, arrived], (0, 1), reg, left, right,
+            source, where, bufs, owners, reg, left, right,
             (tile, nrows, ncols, rows, cols, group),
         )
 
-    merged = lax.cond(over[0] > 0, dense, sparse)
+    merged = lax.cond(over, dense, sparse)
     factor = factor.reshape(1, outer, cols, 1, width, tile).swapaxes(4, 5)
     merged = merged.reshape(1, outer // 2, cols, 1, tile, outer, 1, rows, tile)
     return factor, merged

time: 409 us -> 231 us (0.56)
  waiting for transfers between devices: 138 us -> 43.3 us
  blocking collectives: 65.4 us -> 0 us
  Pallas kernels: 166 us -> 151 us
  between operations: 14.7 us -> 3.63 us
  other arithmetic: 2.42 us -> 9.2 us
    ppermute x15 -> x16, waiting for transfers between devices: 126 us -> 43.3 us  [the longest x1 24.8 us: shards(): far = lax.ppermute(far_move, ('leaf', 'col'), both_pairs)]
    psum x1 -> x0, blocking collectives: 41 us -> none  [shards(): over = lax.psum(over, ('leaf', 'row', 'col'))]
    all_gather x1 -> x0, blocking collectives: 24.4 us -> none  [shards(): reg = lax.all_gather(gains, ('row', 'col'))]
    pallas_call x3 -> x4, Pallas kernels: 101 us -> 84.1 us  [the longest x1 56.7 us: corner_factors(): pl.pallas_call(functools.partial(corner_kernel, (tile, ncols, outer, mine...]
    ppermute x1, waiting for transfers between devices: 12.1 us -> 0.01 us  [shards(): sib_panel = lax.ppermute(own_panel, 'leaf', leaf_pairs)]
    ppermute x15 -> x16, starting transfers between devices: 12.3 us -> 16.9 us  [the longest x6 8.9 us: from_each_col(): lax.ppermute(value, 'col', pairs[k])]
  transfers between devices with their start and end apart: 17 -> 17, of which waited for: 6 -> 7; matrix products, arithmetic and copies ran while one was open for 1% -> 3% of each run, Pallas kernels for 31% -> 49%
where the time goes in v2:
time: 231 us; the launch traced here: 229 us
  Pallas kernels  151 us (65%)
  waiting for transfers between devices  43.3 us (19%)
  starting transfers between devices  18.4 us (8%)
  other arithmetic  9.2 us (4%)
  local copies, waits for them, and re-layouts  3.96 us (2%)
  between operations  3.63 us (2%)
    pallas_call x1, Pallas kernels, corner_factors(): pl.pallas_call(functools.partial(corner_kernel, (tile, ncols, outer, mine...  56.7 us
    pallas_call x1, Pallas kernels, merged_parent(): pl.pallas_call(functools.partial(merge_kernel, dims, leaves), out_shape=j...  37.2 us
    pallas_call x1, Pallas kernels, solved_panels(): pl.pallas_call(functools.partial(solve_kernel, dims), out_shape=[jax.Shap...  29.4 us
    ppermute x1, waiting for transfers between devices, shards(): far = lax.ppermute(far_move, ('leaf', 'col'), both_pairs)  24.8 us
    pallas_call x1, Pallas kernels, sorted_blocks(): pl.pallas_call(functools.partial(sort_kernel, (tile, group, ncols, cap)),...  14.1 us
    pallas_call x1, Pallas kernels, block_flags(): pl.pallas_call(functools.partial(flag_kernel, tile, ncols), out_shape=jax...  11 us
    ppermute x6, starting transfers between devices, from_each_col(): lax.ppermute(value, 'col', pairs[k])  8.9 us
    ppermute x3, waiting for transfers between devices, shards(): crossed = [lax.ppermute(v, 'row', row_pairs) for v in (near, beside, far)]  8.45 us
  transfers between devices with their start and end apart: 17, of which 7 were waited for; matrix products, arithmetic and copies ran while one was open for 3% of the time, Pallas kernels for 49%

profile of v2, /device:TPU:0, one launch (start us, length us, event | category | flops | bytes accessed | tf_op | source)
XLA Modules:
  0.0 229.3 jit_solution(13842120913148371033)
XLA Ops:
  0.6 2.2 panel_and_gains.1
  2.9 2.9 %collective-permute-start.7 = (bf16[2080,128]{1,0:T(8,128)(2,1)}, bf16[2080,128]{1,0:T(8,128)(2,1)S(1)}, u32[]{:S(2)}, u32[]{:S(2)}) collective-permute-start(bf16[2080,128]{1,0:T(8,128)(2,1)} %panel_and_gains.1), channel_id=1, source_target_pairs={{0,1},{1,2},{2,3},{3,0},{4,5},{5,6},{6,7},{7,4},{8,9},{9,10},{10,1... | collective-permute-start | bytes 1597448 | tf_op jit(solution)/shard_map/ppermute | solution.py:600
  5.8 1.5 collective-permute-start.6
  7.3 1.4 collective-permute-start.5
  8.8 1.6 collective-permute-start.4
  10.3 0.4 collective-permute-start.12
  10.9 0.1 reshape.756
  11.0 0.1 reshape.757
  11.1 0.1 reshape.755
  11.2 0.2 compare_reduce_fusion
  11.4 0.2 fusion.26
  11.6 0.1 add_select_fusion.4
  11.7 0.1 reshape.764
  11.8 0.1 reshape.762
  11.9 11.0 %block_flags.1 = f32[8,512]{1,0:T(8,128)} custom-call(bf16[65536,128]{1,0:T(8,128)(2,1)} %bitcast.82), custom_call_target="tpu_custom_call" | custom-call | bytes 30000000 | tf_op jit(solution)/shard_map/block_flags/pallas_call | solution.py:92
  22.9 0.7 compare_reduce_fusion.1
  23.6 0.1 convert_reduce_fusion
  23.8 0.6 reduce_max.31
  25.1 0.6 broadcast_select_fusion.2.entry_ref
  25.6 2.9 %collective-permute-start.8 = (s32[1]{0:T(128)}, s32[1]{0:T(128)}, u32[]{:S(2)}, u32[]{:S(2)}) collective-permute-start(s32[1]{0:T(128)} %bitcast.23), channel_id=1, source_target_pairs={{0,8},{8,0},{16,24},{24,16},{1,9},{9,1},{17,25},{25,17},{2,10},{10... | collective-permute-start | bytes 20 | tf_op jit(solution)/shard_map/ppermute | solution.py:617
  28.5 0.6 collective-permute-done.8
  29.8 1.3 dynamic_update_slice.3
  31.1 0.6 collective-permute-start.11
  31.7 0.5 collective-permute-start.10
  32.2 1.9 collective-permute-start.9
  34.1 0.1 copy.25
  34.2 0.2 fusion.23
  34.5 14.1 %sort_blocks.1 = (bf16[81,128,128]{2,1,0:T(8,128)(2,1)S(1)}, bf16[81,128,128]{2,1,0:T(8,128)(2,1)}, bf16[81,128,128]{2,1,0:T(8,128)(2,1)}, bf16[81,128,128]{2,1,0:T(8,128)(2,1)}, bf16[81,128,128]{2,1,0:T(8,128)(2,1)}) custom-call(s32[512]{0:T(512)} %broadcast_select_fusion.2.entry_ref, bf16[65536,128]{1,0:T(8,128)(2,1)} %bitcast.83), custom_call_target="tpu_custom_call" | custom-call | bytes 60000000 | tf_op jit(solution)/shard_map/sort_blocks/pallas_call | solution.py:175
  48.6 6.3 %collective-permute-done.10 = bf16[2080,128]{1,0:T(8,128)(2,1)} collective-permute-done((bf16[2080,128]{1,0:T(8,128)(2,1)}, bf16[2080,128]{1,0:T(8,128)(2,1)}, u32[]{:S(2)}, u32[]{:S(2)}) %collective-permute-start.10) | collective-permute-done | bytes 532512 | tf_op jit(solution)/shard_map/ppermute | solution.py:600
  54.9 1.6 maximum_bitcast_fusion
  56.4 1.6 maximum_bitcast_fusion.2
  58.0 0.6 pad_maximum_fusion.4.mine_ref
  58.6 2.0 copy-done
  60.6 2.3 %collective-permute-start.15 = (bf16[81,128,128]{2,1,0:T(8,128)(2,1)}, bf16[81,128,128]{2,1,0:T(8,128)(2,1)}, u32[]{:S(2)}, u32[]{:S(2)}) collective-permute-start(bf16[81,128,128]{2,1,0:T(8,128)(2,1)} %get-tuple-element.129), channel_id=1, source_target_pairs={{0,3},{1,0},{2,1},{3,2},{4,7},{5,4},{6,5},{7,6},{8,11},{9,8},{10,9... | collective-permute-start | bytes 7962632 | tf_op jit(solution)/shard_map/ppermute | solution.py:631
  63.0 1.6 collective-permute-start.16
  64.5 0.2 collective-permute-start.17
  64.8 3.2 %collective-permute-done.13.other_ref = bf16[4,2,2080,128]{3,2,1,0:T(8,128)(2,1)} collective-permute-done((bf16[4,2,2080,128]{3,2,1,0:T(8,128)(2,1)S(1)}, bf16[4,2,2080,128]{3,2,1,0:T(8,128)(2,1)}, u32[]{:S(2)}, u32[]{:S(2)}) %collective-permute-start.13) | collective-permute-done | bytes 4259872 | tf_op jit(solution)/shard_map/ppermute | solution.py:634
  68.0 56.7 %corner_factors.1 = (f32[2,256,256]{2,1,0:T(8,128)}, f32[2,256,256]{2,1,0:T(8,128)}) custom-call(s32[3]{0:T(128)S(1)} %pad_add_fusion.1.where_ref, bf16[4,2,2080,128]{3,2,1,0:T(8,128)(2,1)} %copy-done, bf16[4,2,2080,128]{3,2,1,0:T(8,128)(2,1)} %collective-permute-done.13.other_ref), custom_call_target="tpu_custom_call" | custom-call | bytes 200000000 | tf_op jit(solution)/shard_map/corner_factors/pallas_call | solution.py:311
  124.7 29.4 %solve_panels.1 = (f32[32,64,128]{2,1,0:T(8,128)}, bf16[2,16,128,768]{3,2,1,0:T(8,128)(2,1)}, bf16[2,768,2048]{2,1,0:T(8,128)(2,1)}, f32[16,8,128]{2,1,0:T(8,128)S(1)}) custom-call(s32[2,64]{1,0:T(2,128)S(1)} %broadcast_add_fusion.source_ref, s32[3]{0:T(128)S(1)} %pad_add_fusion.1.where_ref, f32[2,256,256]{2,1,0:T(8,128)} %get-tuple-element.124.inverse_ref, ...), custom_call_target="tpu_custom_call" | custom-call | bytes 100000000 | tf_op jit(solution)/shard_map/solve_panels/pallas_call | solution.py:417
  154.2 24.8 %collective-permute-done.17 = bf16[81,128,128]{2,1,0:T(8,128)(2,1)} collective-permute-done((bf16[81,128,128]{2,1,0:T(8,128)(2,1)}, bf16[81,128,128]{2,1,0:T(8,128)(2,1)}, u32[]{:S(2)}, u32[]{:S(2)}) %collective-permute-start.17) | collective-permute-done | bytes 2654240 | tf_op jit(solution)/shard_map/ppermute | solution.py:629
  179.0 0.5 collective-permute-start.19
  179.5 1.3 slice_reduce_fusion.1
  180.8 1.3 slice_reduce_fusion
  183.4 0.9 collective-permute-done.18
  184.3 3.8 %collective-permute-done.19 = bf16[81,128,128]{2,1,0:T(8,128)(2,1)} collective-permute-done((bf16[81,128,128]{2,1,0:T(8,128)(2,1)}, bf16[81,128,128]{2,1,0:T(8,128)(2,1)}, u32[]{:S(2)}, u32[]{:S(2)}) %collective-permute-start.19) | collective-permute-done | bytes 2654240 | tf_op jit(solution)/shard_map/ppermute | solution.py:642
  188.1 3.8 %collective-permute-done.20 = bf16[81,128,128]{2,1,0:T(8,128)(2,1)} collective-permute-done((bf16[81,128,128]{2,1,0:T(8,128)(2,1)}, bf16[81,128,128]{2,1,0:T(8,128)(2,1)}, u32[]{:S(2)}, u32[]{:S(2)}) %collective-permute-start.20) | collective-permute-done | bytes 2654240 | tf_op jit(solution)/shard_map/ppermute | solution.py:642
  191.9 37.2 %conditional.1 = (f32[1,4,4,1,128,8,1,2,128]{8,7,6,5,4,3,2,1,0:T(2,128)}) conditional(s32[]{:T(128)} %convert_element_type.16, (s32[2,64]{1,0:T(2,128)S(1)}, s32[3]{0:T(128)S(1)}, bf16[81,128,128]{2,1,0:T(8,128)(2,1)S(1)}, bf16[81,128,128]{2,1,0:T(8,128)(2,1)}, bf16[81,128,128]{2,1,0:T(8,128)(2,1)}, /*index=5*/bf16[81,128,128]{2,1,0:T(8,128)(2,1)}, ...), branch_computations={%region_5.6_spmd, %region_6.9_spmd} | conditional | flops 83972624 | bytes 503611360 | solution.py:697
  191.9 37.2 %merge_parent.2 = f32[32768,128]{1,0:T(8,128)} custom-call(s32[2,64]{1,0:T(2,128)S(1)} %get-tuple-element.33.source_ref, s32[3]{0:T(128)S(1)} %get-tuple-element.34.where_ref, bf16[81,128,128]{2,1,0:T(8,128)(2,1)S(1)} %get-tuple-element.52.rest_0_, bf16[81,128,128]{2,1,0:T(8,128)(2,1)} %get-tuple-element.53.rest_1_, ...), custom_call_target="tpu_custom_call" | custom-call | tf_op jit(solution)/shard_map/cond/branch_0_fun/merge_parent/pallas_call | solution.py:539
  (29 shorter events, 0.3 us)
Async XLA Ops:
  0.6 9.7 %copy-start.2 = (s32[1,62]{1,0:T(1,128)S(1)}, s32[1,62]{1,0:T(1,128)}, u32[]{:S(2)}) copy-start(s32[1,62]{1,0:T(1,128)} %param.11) | copy-start | bytes 748
  2.9 29.3 %collective-permute-start.7 = (bf16[2080,128]{1,0:T(8,128)(2,1)}, bf16[2080,128]{1,0:T(8,128)(2,1)S(1)}, u32[]{:S(2)}, u32[]{:S(2)}) collective-permute-start(bf16[2080,128]{1,0:T(8,128)(2,1)} %panel_and_gains.1), channel_id=1, source_target_pairs={{0,1},{1,2},{2,3},{3,0},{4,5},{5,6},{6,7},{7,4},{8,9},{9,10},{10,1... | collective-permute-start | bytes 1597448 | tf_op jit(solution)/shard_map/ppermute | solution.py:600
  5.8 42.8 %collective-permute-start.6 = (bf16[2080,128]{1,0:T(8,128)(2,1)}, bf16[2080,128]{1,0:T(8,128)(2,1)}, u32[]{:S(2)}, u32[]{:S(2)}) collective-permute-start(bf16[2080,128]{1,0:T(8,128)(2,1)} %panel_and_gains.1), channel_id=1, source_target_pairs={{0,2},{1,3},{2,0},{3,1},{4,6},{5,7},{6,4},{7,5},{8,10},{9,11},{10,... | collective-permute-start | bytes 1597448 | tf_op jit(solution)/shard_map/ppermute | solution.py:600
  7.3 41.3 %collective-permute-start.5 = (bf16[2080,128]{1,0:T(8,128)(2,1)}, bf16[2080,128]{1,0:T(8,128)(2,1)}, u32[]{:S(2)}, u32[]{:S(2)}) collective-permute-start(bf16[2080,128]{1,0:T(8,128)(2,1)} %panel_and_gains.1), channel_id=1, source_target_pairs={{0,3},{1,0},{2,1},{3,2},{4,7},{5,4},{6,5},{7,6},{8,11},{9,8},{10,9... | collective-permute-start | bytes 1597448 | tf_op jit(solution)/shard_map/ppermute | solution.py:600
  8.8 16.9 %collective-permute-start.4 = (bf16[2080,128]{1,0:T(8,128)(2,1)}, bf16[2080,128]{1,0:T(8,128)(2,1)}, u32[]{:S(2)}, u32[]{:S(2)}) collective-permute-start(bf16[2080,128]{1,0:T(8,128)(2,1)} %panel_and_gains.1), channel_id=1, source_target_pairs={{0,8},{8,0},{16,24},{24,16},{1,9},{9,1},{17,25},{25,17},{2,10},{10... | collective-permute-start | bytes 1597448 | tf_op jit(solution)/shard_map/ppermute | solution.py:604
  10.3 21.4 %collective-permute-start.12 = (s32[62]{0:T(128)S(1)}, s32[62]{0:T(128)S(1)}, u32[]{:S(2)}, u32[]{:S(2)}) collective-permute-start(s32[62]{0:T(128)S(1)} %bitcast.94), channel_id=1, source_target_pairs={{0,8},{8,0},{16,24},{24,16},{1,9},{9,1},{17,25},{25,17},{2,10},{10... | collective-permute-start | bytes 752 | tf_op jit(solution)/shard_map/ppermute | solution.py:605
  25.6 3.5 %collective-permute-start.8 = (s32[1]{0:T(128)}, s32[1]{0:T(128)}, u32[]{:S(2)}, u32[]{:S(2)}) collective-permute-start(s32[1]{0:T(128)} %bitcast.23), channel_id=1, source_target_pairs={{0,8},{8,0},{16,24},{24,16},{1,9},{9,1},{17,25},{25,17},{2,10},{10... | collective-permute-start | bytes 20 | tf_op jit(solution)/shard_map/ppermute | solution.py:617
  31.1 17.5 %collective-permute-start.11 = (bf16[2080,128]{1,0:T(8,128)(2,1)}, bf16[2080,128]{1,0:T(8,128)(2,1)}, u32[]{:S(2)}, u32[]{:S(2)}) collective-permute-start(bf16[2080,128]{1,0:T(8,128)(2,1)} %dynamic_update_slice.3), channel_id=1, source_target_pairs={{0,1},{1,2},{2,3},{3,0},{4,5},{5,6},{6,7},{7,4},{8,9},{9,10},{10,1... | collective-permute-start | bytes 1597448 | tf_op jit(solution)/shard_map/ppermute | solution.py:600
  31.7 23.2 %collective-permute-start.10 = (bf16[2080,128]{1,0:T(8,128)(2,1)}, bf16[2080,128]{1,0:T(8,128)(2,1)}, u32[]{:S(2)}, u32[]{:S(2)}) collective-permute-start(bf16[2080,128]{1,0:T(8,128)(2,1)} %dynamic_update_slice.3), channel_id=1, source_target_pairs={{0,2},{1,3},{2,0},{3,1},{4,6},{5,7},{6,4},{7,5},{8,10},{9,11},{10,... | collective-permute-start | bytes 1597448 | tf_op jit(solution)/shard_map/ppermute | solution.py:600
  32.2 22.7 %collective-permute-start.9 = (bf16[2080,128]{1,0:T(8,128)(2,1)}, bf16[2080,128]{1,0:T(8,128)(2,1)}, u32[]{:S(2)}, u32[]{:S(2)}) collective-permute-start(bf16[2080,128]{1,0:T(8,128)(2,1)} %dynamic_update_slice.3), channel_id=1, source_target_pairs={{0,3},{1,0},{2,1},{3,2},{4,7},{5,4},{6,5},{7,6},{8,11},{9,8},{10,9... | collective-permute-start | bytes 1597448 | tf_op jit(solution)/shard_map/ppermute | solution.py:600
  34.5 20.4 %copy-start.1 = (bf16[2080,128]{1,0:T(8,128)(2,1)S(1)}, bf16[2080,128]{1,0:T(8,128)(2,1)}, u32[]{:S(2)}) copy-start(bf16[2080,128]{1,0:T(8,128)(2,1)} %panel_and_gains.1) | copy-start | bytes 1597444
  58.6 2.0 copy-start
  60.6 7.4 %collective-permute-start.13 = (bf16[4,2,2080,128]{3,2,1,0:T(8,128)(2,1)S(1)}, bf16[4,2,2080,128]{3,2,1,0:T(8,128)(2,1)}, u32[]{:S(2)}, u32[]{:S(2)}) collective-permute-start(bf16[4,2,2080,128]{3,2,1,0:T(8,128)(2,1)S(1)} %pad_maximum_fusion.4.mine_ref), channel_id=1, source_target_pairs={{0,4},{4,0},{1,5},{5,1},{2,6},{6,2},{3,7},{7,3},{8,12},{12,8},{9,1... | collective-permute-start | bytes 12779528 | tf_op jit(solution)/shard_map/ppermute | solution.py:634
  60.6 93.5 %collective-permute-start.15 = (bf16[81,128,128]{2,1,0:T(8,128)(2,1)}, bf16[81,128,128]{2,1,0:T(8,128)(2,1)}, u32[]{:S(2)}, u32[]{:S(2)}) collective-permute-start(bf16[81,128,128]{2,1,0:T(8,128)(2,1)} %get-tuple-element.129), channel_id=1, source_target_pairs={{0,3},{1,0},{2,1},{3,2},{4,7},{5,4},{6,5},{7,6},{8,11},{9,8},{10,9... | collective-permute-start | bytes 7962632 | tf_op jit(solution)/shard_map/ppermute | solution.py:631
  63.0 91.2 %collective-permute-start.16 = (bf16[81,128,128]{2,1,0:T(8,128)(2,1)}, bf16[81,128,128]{2,1,0:T(8,128)(2,1)}, u32[]{:S(2)}, u32[]{:S(2)}) collective-permute-start(bf16[81,128,128]{2,1,0:T(8,128)(2,1)} %get-tuple-element.130), channel_id=1, source_target_pairs={{0,8},{8,0},{16,24},{24,16},{1,9},{9,1},{17,25},{25,17},{2,10},{10... | collective-permute-start | bytes 7962632 | tf_op jit(solution)/shard_map/ppermute | solution.py:630
  64.5 114.4 %collective-permute-start.17 = (bf16[81,128,128]{2,1,0:T(8,128)(2,1)}, bf16[81,128,128]{2,1,0:T(8,128)(2,1)}, u32[]{:S(2)}, u32[]{:S(2)}) collective-permute-start(bf16[81,128,128]{2,1,0:T(8,128)(2,1)} %get-tuple-element.131), channel_id=1, source_target_pairs={{0,11},{1,8},{2,9},{3,10},{8,3},{9,0},{10,1},{11,2},{16,27},{17,24... | collective-permute-start | bytes 7962632 | tf_op jit(solution)/shard_map/ppermute | solution.py:629
  64.8 118.6 %collective-permute-start.14 = (bf16[81,128,128]{2,1,0:T(8,128)(2,1)}, bf16[81,128,128]{2,1,0:T(8,128)(2,1)}, u32[]{:S(2)}, u32[]{:S(2)}) collective-permute-start(bf16[81,128,128]{2,1,0:T(8,128)(2,1)} %get-tuple-element.128), channel_id=1, source_target_pairs={{0,4},{4,0},{1,5},{5,1},{2,6},{6,2},{3,7},{7,3},{8,12},{12,8},{9,1... | collective-permute-start | bytes 7962632 | tf_op jit(solution)/shard_map/ppermute | solution.py:632
  179.0 5.3 %collective-permute-start.18 = (bf16[81,128,128]{2,1,0:T(8,128)(2,1)}, bf16[81,128,128]{2,1,0:T(8,128)(2,1)}, u32[]{:S(2)}, u32[]{:S(2)}) collective-permute-start(bf16[81,128,128]{2,1,0:T(8,128)(2,1)} %collective-permute-done.15), channel_id=1, source_target_pairs={{0,4},{4,0},{1,5},{5,1},{2,6},{6,2},{3,7},{7,3},{8,12},{12,8},{9,1... | collective-permute-start | bytes 7962632 | tf_op jit(solution)/shard_map/ppermute | solution.py:642
  179.0 9.1 %collective-permute-start.19 = (bf16[81,128,128]{2,1,0:T(8,128)(2,1)}, bf16[81,128,128]{2,1,0:T(8,128)(2,1)}, u32[]{:S(2)}, u32[]{:S(2)}) collective-permute-start(bf16[81,128,128]{2,1,0:T(8,128)(2,1)} %collective-permute-done.16), channel_id=1, source_target_pairs={{0,4},{4,0},{1,5},{5,1},{2,6},{6,2},{3,7},{7,3},{8,12},{12,8},{9,1... | collective-permute-start | bytes 7962632 | tf_op jit(solution)/shard_map/ppermute | solution.py:642
  179.5 12.4 %collective-permute-start.20 = (bf16[81,128,128]{2,1,0:T(8,128)(2,1)}, bf16[81,128,128]{2,1,0:T(8,128)(2,1)}, u32[]{:S(2)}, u32[]{:S(2)}) collective-permute-start(bf16[81,128,128]{2,1,0:T(8,128)(2,1)} %collective-permute-done.17), channel_id=1, source_target_pairs={{0,4},{4,0},{1,5},{5,1},{2,6},{6,2},{3,7},{7,3},{8,12},{12,8},{9,1... | collective-permute-start | bytes 7962632 | tf_op jit(solution)/shard_map/ppermute | solution.py:642

commit v3 on v2

--- a/solution.py
+++ b/solution.py
@@ -9,7 +9,7 @@
 
 NPAN = 1
 VMEM_LIMIT = 60 * 1024 * 1024
-CLASSES = 5
+PART = 8
 f32 = jnp.float32
 bf16 = jnp.bfloat16
 i32 = jnp.int32
@@ -92,8 +92,8 @@
     return pl.pallas_call(
         functools.partial(flag_kernel, tile, ncols),
         out_shape=jax.ShapeDtypeStruct((8, count), f32),
-        grid=(nrows // 4,),
-        in_specs=[pl.BlockSpec((4 * tile * ncols, tile), lambda i: (i, 0))],
+        grid=(nrows // 8,),
+        in_specs=[pl.BlockSpec((8 * tile * ncols, tile), lambda i: (i, 0))],
         out_specs=pl.BlockSpec((8, count), lambda i: (0, 0)),
         scratch_shapes=[pltpu.VMEM((count, tile), f32)],
         compiler_params=pltpu.CompilerParams(vmem_limit_bytes=VMEM_LIMIT),
@@ -103,9 +103,10 @@
 
 
 def sort_kernel(dims, entry_ref, x_ref, *rest):
-    tile, group, ncols, cap = dims
-    bufs = rest[:CLASSES]
-    wide, blocks, lists, lists_low, counts, sem = rest[CLASSES:]
+    tile, group, ncols, rows, rooms = dims
+    regions = len(rooms)
+    bufs = rest[:regions]
+    wide, blocks, lists, lists_low, counts, sem = rest[regions:]
     step = pl.program_id(0)
     lines = tile * ncols
     lane = lax.broadcasted_iota(i32, (8, tile), 1)
@@ -114,7 +115,7 @@
     @pl.when(step == 0)
     def _():
         lists[...] = jnp.zeros_like(lists)
-        for k in range(CLASSES):
+        for k in range(regions * 2):
             counts[k] = 0
 
     for g in range(group):
@@ -128,17 +129,27 @@
             @pl.when(entry >= 0)
             def _():
                 kind = entry % 8
-                code = entry // 8
-                slot = counts[kind]
-                counts[kind] = slot + 1
-                blocks[at] = wide[g, pl.ds(j, tile, stride=ncols), :].astype(bf16)
-                here = jnp.where(sublane == 0, code // 256, code % 256).astype(f32)
-                lists[kind] = jnp.where(lane == slot, here, lists[kind])
-                for k in range(CLASSES):
-
-                    @pl.when((kind == k) & (slot < cap))
-                    def _():
-                        pltpu.make_async_copy(blocks.at[at], bufs[k].at[slot], sem).start()
+                end = entry // 8 % rows
+                code = entry // (8 * rows)
+                held = counts[kind * 2] + counts[kind * 2 + 1]
+                spills = (kind >= 2) & (held >= rooms[2])
+                region = jnp.where(spills, kind + 3, kind)
+                room = jnp.where(spills, rooms[5], jnp.where(kind >= 2, rooms[2], rooms[0]))
+                front = counts[region * 2]
+                back = counts[region * 2 + 1]
+                slot = jnp.where(end == 0, front, room - 1 - back)
+
+                @pl.when(front + back < room)
+                def _():
+                    counts[region * 2 + end] = jnp.where(end == 0, front, back) + 1
+                    blocks[at] = wide[g, pl.ds(j, tile, stride=ncols), :].astype(bf16)
+                    here = jnp.where(sublane == 0, code // 256, code % 256).astype(f32)
+                    lists[region] = jnp.where(lane == slot, here, lists[region])
+                    for k in range(regions):
+
+                        @pl.when(region == k)
+                        def _():
+                            pltpu.make_async_copy(blocks.at[at], bufs[k].at[slot], sem).start()
 
         return carry
 
@@ -147,14 +158,16 @@
     @pl.when(step == pl.num_programs(0) - 1)
     def _():
         sent = 0
-        for k in range(CLASSES):
-            taken = jnp.minimum(counts[k], cap)
-            sent = sent + taken
-            listed = jnp.where(sublane == 2, taken.astype(f32), lists[k])
+        for k in range(regions):
+            front = counts[2 * k]
+            back = counts[2 * k + 1]
+            sent = sent + front + back
+            listed = jnp.where(sublane == 2, front.astype(f32), lists[k])
+            listed = jnp.where(sublane == 3, back.astype(f32), listed)
             lists_low[k] = jnp.concatenate([listed, listed], axis=0).astype(bf16)
         copies = [
-            pltpu.make_async_copy(lists_low.at[k], bufs[k].at[cap, pl.ds(0, 16)], sem)
-            for k in range(CLASSES)
+            pltpu.make_async_copy(lists_low.at[k], bufs[k].at[rooms[k], pl.ds(0, 16)], sem)
+            for k in range(regions)
         ]
         for copy in copies:
             copy.start()
@@ -169,21 +182,23 @@
 
 
 def sorted_blocks(x, entries, dims):
-    tile, nrows, ncols, cap = dims
+    tile, nrows, ncols, rows, rooms = dims
     group = 4
-    smem = pl.BlockSpec(memory_space=pltpu.SMEM)
     return pl.pallas_call(
-        functools.partial(sort_kernel, (tile, group, ncols, cap)),
-        out_shape=[jax.ShapeDtypeStruct((cap + 1, tile, tile), bf16)] * CLASSES,
+        functools.partial(sort_kernel, (tile, group, ncols, rows, rooms)),
+        out_shape=[jax.ShapeDtypeStruct((room + 1, tile, tile), bf16) for room in rooms],
         grid=(nrows // group,),
-        in_specs=[smem, pl.BlockSpec((group * tile * ncols, tile), lambda i: (i, 0))],
-        out_specs=[pl.BlockSpec(memory_space=pl.ANY)] * CLASSES,
+        in_specs=[
+            pl.BlockSpec(memory_space=pltpu.SMEM),
+            pl.BlockSpec((group * tile * ncols, tile), lambda i: (i, 0)),
+        ],
+        out_specs=[pl.BlockSpec(memory_space=pl.ANY)] * len(rooms),
         scratch_shapes=[
             pltpu.VMEM((group, tile * ncols, tile), f32),
             pltpu.VMEM((nrows * ncols, tile, tile), bf16),
-            pltpu.VMEM((CLASSES, 8, tile), f32),
-            pltpu.VMEM((CLASSES, 16, tile), bf16),
-            pltpu.SMEM((CLASSES,), i32),
+            pltpu.VMEM((len(rooms), 8, tile), f32),
+            pltpu.VMEM((len(rooms), 16, tile), bf16),
+            pltpu.SMEM((len(rooms) * 2,), i32),
             pltpu.SemaphoreType.DMA,
         ],
         compiler_params=pltpu.CompilerParams(vmem_limit_bytes=VMEM_LIMIT),
@@ -319,7 +334,7 @@
             pltpu.VMEM((2, 2, tail, tile), bf16),
             pltpu.SemaphoreType.DMA((2, 2)),
         ],
-        cost_estimate=pl.CostEstimate(flops=0, bytes_accessed=200_000_000, transcendentals=0),
+        cost_estimate=pl.CostEstimate(flops=0, bytes_accessed=60_000_000, transcendentals=0),
         name="corner_factors",
     )(where, mine, other)
 
@@ -429,7 +444,7 @@
             pltpu.SemaphoreType.DMA,
         ],
         compiler_params=pltpu.CompilerParams(vmem_limit_bytes=VMEM_LIMIT),
-        cost_estimate=pl.CostEstimate(flops=0, bytes_accessed=100_000_000, transcendentals=0),
+        cost_estimate=pl.CostEstimate(flops=0, bytes_accessed=1_000_000, transcendentals=0),
         name="solve_panels",
     )(source, where, inverse, upper, mine, other)
 
@@ -439,7 +454,7 @@
     count = len(leaves)
     bufs = rest[:count]
     reg_ref, left_ref, right_ref, out_ref = rest[count : count + 4]
-    table, blocks, totals, lists_low, lists_v, lists, sem = rest[count + 4 :]
+    table, blocks, lists_low, lists_v, lists, sem = rest[count + 4 :]
     step = pl.program_id(0)
     side = where_ref[0]
     row_at = where_ref[1]
@@ -461,42 +476,74 @@
         ]
         for copy in copies:
             copy.start()
-        lax.fori_loop(0, 2 * per_leaf, clear, 0)
+        lax.fori_loop(0, 2 * per_leaf, clear, 0, unroll=16)
         blocks[0] = jnp.zeros((tile, tile), bf16)
-        filled = 1
         for copy in copies:
             copy.wait()
         for k in range(count):
             listed = lists_low[k].astype(f32)
             codes = listed[0:1] * 256.0 + listed[1:2]
-            lists_v[k] = jnp.concatenate([codes, listed[2:3]] + [codes] * 6, axis=0).astype(i32)
+            lists_v[k] = jnp.concatenate([codes, listed[2:4]] + [codes] * 5, axis=0).astype(i32)
         copy = pltpu.make_async_copy(lists_v, lists, sem)
         copy.start()
         copy.wait()
+        base = 1
+        started = 0
         for k in range(count):
-
-            def place(e, slot):
-                code = lists[k, 0, e]
-                mine = code % rows == row_at
-
-                @pl.when(mine)
-                def _():
-                    table[leaves[k] * per_leaf + code // rows] = slot
-                    pltpu.make_async_copy(bufs[k].at[e], blocks.at[slot], sem).start()
-
-                return slot + jnp.where(mine, 1, 0)
-
-            filled = lax.fori_loop(0, lists[k, 1, 0], place, filled)
+            room = bufs[k].shape[0] - 1
+            mine = lists[k, 1 + row_at, 0]
+            first = jnp.where(row_at == 0, 0, room - mine)
+            parts = lax.div(mine + (PART - 1), PART)
+
+            def fetch(c, carry):
+                at = jnp.where(row_at == 0, c * PART, room - PART - c * PART)
+                pltpu.make_async_copy(
+                    bufs[k].at[pl.ds(at, PART)], blocks.at[pl.ds(base + at, PART)], sem
+                ).start()
+                return carry
+
+            lax.fori_loop(0, parts, fetch, 0)
+
+            def place(e, carry):
+                table[leaves[k] * per_leaf + lists[k, 0, e]] = base + e
+                return carry
+
+            lax.fori_loop(first, first + mine, place, 0)
+            base = base + room
+            started = started + parts
 
         def drain(_, carry):
-            pltpu.make_async_copy(bufs[0].at[0], blocks.at[0], sem).wait()
+            pltpu.make_async_copy(
+                bufs[0].at[pl.ds(0, PART)], blocks.at[pl.ds(1, PART)], sem
+            ).wait()
             return carry
 
-        lax.fori_loop(1, filled, drain, 0)
-
-    for leaf in range(2):
-        left = left_ref[leaf].reshape(group * tile, left_ref.shape[-1])
-        totals[leaf] = jnp.dot(left, right_ref[leaf], preferred_element_type=f32)
+        lax.fori_loop(0, started, drain, 0)
+
+    def less(slot, update):
+        return (blocks[slot].astype(f32) - update).astype(bf16).astype(f32)
+
+    wide = min(2, ncols)
+    lefts = [left_ref[leaf].reshape(group * tile, left_ref.shape[-1]) for leaf in range(2)]
+    for first in range(0, ncols, wide):
+        updates = [
+            jnp.dot(
+                lefts[leaf],
+                right_ref[leaf, :, first * tile : (first + wide) * tile],
+                preferred_element_type=f32,
+            )
+            for leaf in range(2)
+        ]
+        for g in range(group):
+            for w in range(wide):
+                j = first + w
+                parts = []
+                for leaf in range(2):
+                    slot = table[leaf * per_leaf + (step * group + g) * ncols + j]
+                    update = updates[leaf][g * tile : (g + 1) * tile, w * tile : (w + 1) * tile]
+                    parts.append(less(slot, update))
+                out_ref[pl.ds(g * tile * ncols + j, tile, stride=ncols), :] = parts[0] + parts[1]
+
     on_diagonal = lax.broadcasted_iota(i32, (tile, tile), 0) == lax.broadcasted_iota(
         i32, (tile, tile), 1
     )
@@ -507,25 +554,19 @@
         @pl.when(parent // rows % cols == col_at)
         def _():
             j = parent // (rows * cols) * rows + parent % rows
-            lanes = pl.ds(pl.multiple_of(j * tile, tile), tile)
+            parts = []
             for leaf in range(2):
                 block = source_ref[leaf, parent]
-
-                @pl.when(block >= 0)
-                def _():
-                    at = (block % rows * cols + block // rows % cols) * 2 + leaf
-                    gain = reg_ref[at, pl.ds(block // (rows * cols), 1), :]
-                    here = totals[leaf, g * tile : (g + 1) * tile, lanes]
-                    totals[leaf, g * tile : (g + 1) * tile, lanes] = here - jnp.where(
-                        on_diagonal, gain, 0.0
-                    )
-
-        for j in range(ncols):
-            parts = []
-            for leaf in range(2):
-                slot = table[leaf * per_leaf + place_row * ncols + j]
-                total = totals[leaf, g * tile : (g + 1) * tile, j * tile : (j + 1) * tile]
-                parts.append((blocks[slot].astype(f32) - total).astype(bf16).astype(f32))
+                present = jnp.maximum(block, 0)
+                at = (present % rows * cols + present // rows % cols) * 2 + leaf
+                gain = reg_ref[at, pl.ds(present // (rows * cols), 1), :]
+                gain = jnp.where(on_diagonal & (block >= 0), gain, 0.0)
+                update = jnp.dot(
+                    left_ref[leaf, g],
+                    right_ref[leaf, :, pl.ds(pl.multiple_of(j * tile, tile), tile)],
+                    preferred_element_type=f32,
+                )
+                parts.append(less(table[leaf * per_leaf + place_row * ncols + j], update - gain))
             out_ref[pl.ds(g * tile * ncols + j, tile, stride=ncols), :] = parts[0] + parts[1]
 
 
@@ -550,8 +591,7 @@
         out_specs=pl.BlockSpec((group * tile * ncols, tile), lambda i: (i, 0)),
         scratch_shapes=[
             pltpu.SMEM((nrows * ncols,), i32),
-            pltpu.VMEM((nrows * ncols + 1, tile, tile), bf16),
-            pltpu.VMEM((2, group * tile, ncols * tile), f32),
+            pltpu.VMEM((1 + sum(buf.shape[0] - 1 for buf in bufs), tile, tile), bf16),
             pltpu.VMEM((count, 16, tile), bf16),
             pltpu.VMEM((count, 8, tile), i32),
             pltpu.SMEM((count, 8, tile), i32),
@@ -581,7 +621,9 @@
     nrows = outer * cols
     ncols = outer * rows
     blocks = nrows * rows
-    cap = nrows * ncols * 5 // 32
+    cap = -(-nrows * ncols * 5 // 256) * 8
+    spill = -(-cap // (5 * PART)) * PART
+    rooms = (cap,) * 2 + (cap - spill,) * 3 + (spill,) * 3
     width = NPAN * rows * tile // cols
     group = 2
     where = jnp.stack([side, row_at, col_at]).astype(i32)
@@ -604,28 +646,34 @@
     sib_panel = lax.ppermute(own_panel, "leaf", leaf_pairs)
     sib_map = lax.ppermute(own_map, "leaf", leaf_pairs)
     own_panels = from_each_col(own_panel)
-    maps = jnp.stack([own_map, sib_map])
-    source = sparse_sources(maps, blocks, NPAN * rows)
-
     hits = block_flags(flat, tile, nrows, ncols)
     moves = block_moves(own_map, side, row_at, col_at, nrows, ncols, rows, cols)
     entries = jnp.where(hits[0] > 0, moves, -1)
-    kinds = jnp.arange(CLASSES, dtype=i32)[:, None]
+    kinds = jnp.arange(5, dtype=i32)[:, None]
     counts = jnp.sum(((entries >= 0)[None, :] & (entries % 8 == kinds)).astype(i32), axis=1)
-    over = jnp.max(counts, keepdims=True) - cap
-    sib_panel, entries, over = lax.optimization_barrier((sib_panel, entries, over))
-    over = jnp.maximum(over, lax.ppermute(over, "leaf", leaf_pairs))
-    mark = jnp.where(over > 0, 1.0, 0.0).astype(bf16)
+    first_room = cap - spill
+    stats = jnp.stack(
+        [
+            jnp.max(counts) > cap,
+            jnp.maximum(counts[2], counts[4]) > first_room,
+            counts[3] > first_room,
+        ]
+    ).astype(i32)
+    sib_panel, sib_map, entries, stats = lax.optimization_barrier(
+        (sib_panel, sib_map, entries, stats)
+    )
+    stats = jnp.maximum(stats, lax.ppermute(stats, "leaf", leaf_pairs))
     mark_row = own_panel.shape[0] - 1
-    sib_panel = lax.dynamic_update_slice(
-        sib_panel, jnp.broadcast_to(mark[:, None], (1, tile)), (mark_row, 0)
-    )
+    mark = jnp.pad(stats.astype(bf16), (0, tile - 3))[None, :]
+    sib_panel = lax.dynamic_update_slice(sib_panel, mark, (mark_row, 0))
     sib_panels = from_each_col(sib_panel)
-    found = sorted_blocks(flat, entries, (tile, nrows, ncols, cap))
+    maps = jnp.stack([own_map, sib_map])
+    source = sparse_sources(maps, blocks, NPAN * rows)
+    found = sorted_blocks(flat, entries, (tile, nrows, ncols, rows, rooms))
     found, own_panels, sib_panels, source = lax.optimization_barrier(
         (found, own_panels, sib_panels, source)
     )
-    kept, row_move, col_move, leaf_move, far_move = found
+    kept, row_move, col_move, leaf_move, far_move, col_more, leaf_more, far_more = found
     far = lax.ppermute(far_move, ("leaf", "col"), both_pairs)
     beside = lax.ppermute(leaf_move, "leaf", leaf_pairs)
     near = lax.ppermute(col_move, "col", col_pairs)
@@ -636,12 +684,37 @@
     factor, left, right, reg = solved_panels(
         source, where, inverse, upper, mine, other, (tile, nrows, ncols, rows, cols, width)
     )
-    marks = jnp.concatenate([mine[:, 1, mark_row, 0], other[:, 1, mark_row, 0]])
-    over = jnp.max(marks.astype(f32)) > 0
-    near, beside, far, left, right = lax.optimization_barrier((near, beside, far, left, right))
-    crossed = [lax.ppermute(v, "row", row_pairs) for v in (near, beside, far)]
-    bufs = [kept, across, near, beside, far] + crossed
-    owners = (0, 0, 0, 1, 1, 0, 1, 1)
+    marks = jnp.concatenate([mine[:, 1, mark_row, :3], other[:, 1, mark_row, :3]])
+    marks = jnp.max(marks.astype(f32), axis=0) > 0
+    near, beside, far, left, right, marks = lax.optimization_barrier(
+        (near, beside, far, left, right, marks)
+    )
+    over = marks[0]
+
+    def rest_of(cols_too, leaves_too):
+        def branch(near, beside, far, col_more, leaf_more, far_more):
+            if cols_too:
+                far_more = lax.ppermute(far_more, ("leaf", "col"), both_pairs)
+                col_more = lax.ppermute(col_more, "col", col_pairs)
+            if leaves_too:
+                leaf_more = lax.ppermute(leaf_more, "leaf", leaf_pairs)
+            firsts = [lax.ppermute(v, "row", row_pairs) for v in (near, beside, far)]
+            more = [col_more, leaf_more, far_more]
+            crossed = [
+                lax.ppermute(v, "row", row_pairs) if sent else v
+                for v, sent in zip(more, (cols_too, leaves_too, cols_too))
+            ]
+            return firsts, more, crossed
+
+        return branch
+
+    firsts, more, crossed = lax.switch(
+        marks[1].astype(i32) * 2 + marks[2].astype(i32),
+        [rest_of(i // 2 == 1, i % 2 == 1) for i in range(4)],
+        near, beside, far, col_more, leaf_more, far_more,
+    )
+    bufs = [kept, across, near, beside, far] + firsts + more + crossed
+    owners = (0, 0) + (0, 1, 1) * 4
 
     def sparse():
         return merged_parent(
@@ -684,9 +757,10 @@
         bufs = []
         for value in (stays, arrived):
             for first in range(0, every, part):
-                codes = (first + jnp.arange(tile, dtype=i32)) * rows + row_at
-                listed = jnp.stack([codes // 256, codes % 256, jnp.full((tile,), part, i32)])
-                listed = jnp.pad(listed, ((0, tile - 3), (0, 0))).astype(bf16)
+                codes = first + jnp.arange(tile, dtype=i32)
+                full = jnp.full((tile,), part, i32)
+                listed = jnp.stack([codes // 256, codes % 256, full, full])
+                listed = jnp.pad(listed, ((0, tile - 4), (0, 0))).astype(bf16)
                 bufs.append(jnp.concatenate([value[first : first + part], listed[None]]))
         owners = (0,) * (len(bufs) // 2) + (1,) * (len(bufs) // 2)
         return merged_parent(

time: 231 us -> 204 us (0.88)
  waiting for transfers between devices: 43.3 us -> 19.5 us
  Pallas kernels: 151 us -> 146 us
  local copies, waits for them, and re-layouts: 3.96 us -> 7.2 us
    ppermute x1, waiting for transfers between devices: 24.8 us -> 1.67 us  [shards(): far = lax.ppermute(far_move, ('leaf', 'col'), both_pairs)]
    pallas_call x1, Pallas kernels: 37.2 us -> 29.2 us  [merged_parent(): pl.pallas_call(functools.partial(merge_kernel, dims, leaves), out_shape=j...]
    ppermute x6, waiting for transfers between devices: 6.27 us -> 1.35 us  [from_each_col(): lax.ppermute(value, 'col', pairs[k])]
    pallas_call x1, Pallas kernels: 14.1 us -> 18.9 us  [sorted_blocks(): pl.pallas_call(functools.partial(sort_kernel, (tile, group, ncols, rows,...]
    ppermute x1, waiting for transfers between devices: 0.01 us -> 4.45 us  [shards(): across = lax.ppermute(row_move, 'row', row_pairs)]
    cond x0 -> x5, local copies, waits for them, and re-layouts: none -> 3.96 us
  transfers between devices with their start and end apart: 17 -> 17, of which waited for: 7 -> 8; matrix products, arithmetic and copies ran while one was open for 3% -> 4% of each run, Pallas kernels for 49% -> 56%
where the time goes in v3:
time: 204 us; the launch traced here: 203 us
  Pallas kernels  146 us (72%)
  waiting for transfers between devices  19.5 us (10%)
  starting transfers between devices  18.2 us (9%)
  local copies, waits for them, and re-layouts  7.2 us (4%)
  other arithmetic  7.08 us (3%)
  between operations  5.35 us (3%)
    pallas_call x1, Pallas kernels, corner_factors(): pl.pallas_call(functools.partial(corner_kernel, (tile, ncols, outer, mine...  56.7 us
    pallas_call x1, Pallas kernels, solved_panels(): pl.pallas_call(functools.partial(solve_kernel, dims), out_shape=[jax.Shap...  29.4 us
    pallas_call x1, Pallas kernels, merged_parent(): pl.pallas_call(functools.partial(merge_kernel, dims, leaves), out_shape=j...  29.2 us
    pallas_call x1, Pallas kernels, sorted_blocks(): pl.pallas_call(functools.partial(sort_kernel, (tile, group, ncols, rows,...  18.9 us
    pallas_call x1, Pallas kernels, block_flags(): pl.pallas_call(functools.partial(flag_kernel, tile, ncols), out_shape=jax...  9.4 us
    ppermute x6, starting transfers between devices, from_each_col(): lax.ppermute(value, 'col', pairs[k])  8.9 us
    ppermute x3, waiting for transfers between devices, branch(): firsts = [lax.ppermute(v, 'row', row_pairs) for v in (near, beside, far)]  7.58 us
    ppermute x1, waiting for transfers between devices, shards(): across = lax.ppermute(row_move, 'row', row_pairs)  4.45 us
  transfers between devices with their start and end apart: 17, of which 8 were waited for; matrix products, arithmetic and copies ran while one was open for 4% of the time, Pallas kernels for 56%

profile of v3, /device:TPU:0, one launch (start us, length us, event | category | flops | bytes accessed | tf_op | source)
XLA Modules:
  0.0 203.1 jit_solution(151463700885283280)
XLA Ops:
  0.6 2.2 %panel_and_gains.1 = bf16[2080,128]{1,0:T(8,128)(2,1)} custom-call(bf16[65536,128]{1,0:T(8,128)(2,1)} %bitcast.83, f32[8,128]{1,0:T(8,128)} %bitcast.97), custom_call_target="tpu_custom_call" | custom-call | tf_op jit(solution)/shard_map/panel_and_gains/pallas_call | solution.py:51
  2.9 2.9 %collective-permute-start.32 = (bf16[2080,128]{1,0:T(8,128)(2,1)}, bf16[2080,128]{1,0:T(8,128)(2,1)S(1)}, u32[]{:S(2)}, u32[]{:S(2)}) collective-permute-start(bf16[2080,128]{1,0:T(8,128)(2,1)} %panel_and_gains.1), channel_id=1, source_target_pairs={{0,1},{1,2},{2,3},{3,0},{4,5},{5,6},{6,7},{7,4},{8,9},{9,10},{10,1... | collective-permute-start | bytes 1597448 | tf_op jit(solution)/shard_map/ppermute | solution.py:642
  5.8 1.5 collective-permute-start.31
  7.3 1.4 collective-permute-start.30
  8.8 1.6 collective-permute-start.28
  10.3 0.4 collective-permute-start.29
  11.2 0.2 compare_reduce_fusion
  11.4 0.2 fusion.26
  11.9 9.4 %block_flags.1 = f32[8,512]{1,0:T(8,128)} custom-call(bf16[65536,128]{1,0:T(8,128)(2,1)} %bitcast.84), custom_call_target="tpu_custom_call" | custom-call | bytes 30000000 | tf_op jit(solution)/shard_map/block_flags/pallas_call | solution.py:92
  21.3 0.7 compare_reduce_fusion.1
  22.0 0.1 convert_reduce_fusion
  22.1 0.6 reduce_max.31
  22.8 0.6 broadcast_select_fusion.2.entry_ref
  23.4 0.6 fusion.42
  26.6 1.6 collective-permute-start.33
  28.2 2.0 collective-permute-done.33
  30.2 1.3 dynamic_update_slice.3
  31.4 0.6 collective-permute-start.36
  32.0 0.5 collective-permute-start.35
  32.5 1.9 collective-permute-start.34
  34.6 18.9 %sort_blocks.1 = (bf16[81,128,128]{2,1,0:T(8,128)(2,1)}, bf16[81,128,128]{2,1,0:T(8,128)(2,1)}, bf16[65,128,128]{2,1,0:T(8,128)(2,1)}, bf16[65,128,128]{2,1,0:T(...) custom-call(s32[512]{0:T(512)} %broadcast_select_fusion.2.entry_ref,, ...), custom_call_target="tpu_custom_call" | custom-call | bytes 60000000 | tf_op jit(solution)/shard_map/sort_blocks/pallas_call | solution.py:187
  53.5 0.2 fusion.23
  53.7 1.3 collective-permute-done.35
  55.1 1.4 maximum_bitcast_fusion
  56.5 1.4 maximum_bitcast_fusion.2
  57.9 0.6 pad_maximum_fusion.4.mine_ref
  58.5 2.4 %collective-permute-start.38 = (bf16[65,128,128]{2,1,0:T(8,128)(2,1)}, bf16[65,128,128]{2,1,0:T(8,128)(2,1)}, u32[]{:S(2)}, u32[]{:S(2)}) collective-permute-start(bf16[65,128,128]{2,1,0:T(8,128)(2,1)} %get-tuple-element.238), channel_id=1, source_target_pairs={{0,3},{1,0},{2,1},{3,2},{4,7},{5,4},{6,5},{7,6},{8,11},{9,8},{10,9... | collective-permute-start | bytes 6389768 | tf_op jit(solution)/shard_map/ppermute | solution.py:679
  60.9 1.6 collective-permute-start.39
  62.5 0.8 collective-permute-start.40
  63.4 2.5 %collective-permute-done.37.other_ref = bf16[4,2,2080,128]{3,2,1,0:T(8,128)(2,1)} collective-permute-done((bf16[4,2,2080,128]{3,2,1,0:T(8,128)(2,1)S(1)}, bf16[4,2,2080,128]{3,2,1,0:T(8,128)(2,1)}, u32[]{:S(2)}, u32[]{:S(2)}) %collective-permute-start.37) | collective-permute-done | bytes 4259872 | tf_op jit(solution)/shard_map/ppermute | solution.py:682
  65.9 56.7 %corner_factors.1 = (f32[2,256,256]{2,1,0:T(8,128)}, f32[2,256,256]{2,1,0:T(8,128)}) custom-call(s32[3]{0:T(128)S(1)} %pad_add_fusion.1.where_ref, bf16[4,2,2080,128]{3,2,1,0:T(8,128)(2,1)} %copy-done, bf16[4,2,2080,128]{3,2,1,0:T(8,128)(2,1)} %collective-permute-done.37.other_ref), custom_call_target="tpu_custom_call" | custom-call | bytes 60000000 | tf_op jit(solution)/shard_map/corner_factors/pallas_call | solution.py:326
  122.6 29.4 %solve_panels.1 = (f32[32,64,128]{2,1,0:T(8,128)}, bf16[2,16,128,768]{3,2,1,0:T(8,128)(2,1)}, bf16[2,768,2048]{2,1,0:T(8,128)(2,1)}, f32[16,8,128]{2,1,0:T(8,128)S(1)}) custom-call(s32[2,64]{1,0:T(2,128)S(1)} %broadcast_add_fusion.source_ref, s32[3]{0:T(128)S(1)} %pad_add_fusion.1.where_ref, f32[2,256,256]{2,1,0:T(8,128)} %get-tuple-element.235.inverse_ref, ...), custom_call_target="tpu_custom_call" | custom-call | bytes 1000000 | tf_op jit(solution)/shard_map/solve_panels/pallas_call | solution.py:432
  152.0 0.7 slice_reduce_fusion
  152.7 1.7 collective-permute-done.40
  154.4 0.6 fusion.41
  156.4 10.7 %conditional.2 = (bf16[65,128,128]{2,1,0:T(8,128)(2,1)}, bf16[65,128,128]{2,1,0:T(8,128)(2,1)}, bf16[65,128,128]{2,1,0:T(8,128)(2,1)}, bf16[17,128,128]{2,1,0:T(...) conditional(s32[]{:T(128)} %bitcast.45, ...), branch_computations={%region_5.6_spmd, %region_6.7_spmd, %region_7.8_spmd, %region_8.9_... | conditional | bytes 42271152 | solution.py:711
  156.5 0.5 collective-permute-start.1
  157.1 0.8 copy.47
  157.9 0.8 copy.48
  158.7 0.9 copy.49
  159.5 1.5 collective-permute-done
  161.0 3.0 %collective-permute-done.1 = bf16[65,128,128]{2,1,0:T(8,128)(2,1)} collective-permute-done((bf16[65,128,128]{2,1,0:T(8,128)(2,1)}, bf16[65,128,128]{2,1,0:T(8,128)(2,1)}, u32[]{:S(2)}, u32[]{:S(2)}) %collective-permute-start.1) | collective-permute-done | bytes 2129952 | tf_op jit(solution)/shard_map/cond/branch_0_fun/ppermute | solution.py:701
  164.1 3.0 %collective-permute-done.2 = bf16[65,128,128]{2,1,0:T(8,128)(2,1)} collective-permute-done((bf16[65,128,128]{2,1,0:T(8,128)(2,1)}, bf16[65,128,128]{2,1,0:T(8,128)(2,1)}, u32[]{:S(2)}, u32[]{:S(2)}) %collective-permute-start.2) | collective-permute-done | bytes 2129952 | tf_op jit(solution)/shard_map/cond/branch_0_fun/ppermute | solution.py:701
  167.1 0.1 collective-permute-start.41
  167.8 4.4 %collective-permute-done.41 = bf16[81,128,128]{2,1,0:T(8,128)(2,1)S(1)} collective-permute-done((bf16[81,128,128]{2,1,0:T(8,128)(2,1)}, bf16[81,128,128]{2,1,0:T(8,128)(2,1)S(1)}, u32[]{:S(2)}, u32[]{:S(2)}) %collective-permute-start.41) | collective-permute-done | bytes 2654240 | tf_op jit(solution)/shard_map/ppermute | solution.py:680
  172.3 30.7 %conditional.3 = (f32[1,4,4,1,128,8,1,2,128]{8,7,6,5,4,3,2,1,0:T(2,128)}) conditional(s32[]{:T(128)} %bitcast.44, (s32[2,64]{1,0:T(2,128)S(1)}, s32[3]{0:T(128)S(1)}, bf16[81,128,128]{2,1,0:T(8,128)(2,1)}, bf16[81,128,128]{2,1,0:T(8,128)(2,1)S(1)}, bf16[65,128,128]{2,1,0:T(8,128)(2,1)}, /*index=5*/bf16[65,128,128]{2,1,0:T(8,128)(2,1)}, ...), branch_computations={%region_9.10_spmd, %region_10.13_spmd} | conditional | flops 83971472 | bytes 503612384 | solution.py:771
  172.3 1.5 copy-done.1
  173.8 29.2 %merge_parent.2 = f32[32768,128]{1,0:T(8,128)} custom-call(s32[2,64]{1,0:T(2,128)S(1)} %get-tuple-element.134.source_ref, s32[3]{0:T(128)S(1)} %get-tuple-element.135.where_ref, bf16[81,128,128]{2,1,0:T(8,128)(2,1)} %get-tuple-element.136.rest_0_, bf16[81,128,128]{2,1,0:T(8,128)(2,1)} %copy-done.1, bf16[65,128,128]{2,1,0:T(8,128)(2,1)} %get-tuple-element.138.rest_2_, ...), custom_call_target="tpu_custom_call" | custom-call | tf_op jit(solution)/shard_map/cond/branch_0_fun/merge_parent/pallas_call | solution.py:580
  (40 shorter events, 1.3 us)
Async XLA Ops:
  0.6 9.7 %copy-start.3 = (s32[1,62]{1,0:T(1,128)S(1)}, s32[1,62]{1,0:T(1,128)}, u32[]{:S(2)}) copy-start(s32[1,62]{1,0:T(1,128)} %param.15) | copy-start | bytes 748
  2.9 29.7 %collective-permute-start.32 = (bf16[2080,128]{1,0:T(8,128)(2,1)}, bf16[2080,128]{1,0:T(8,128)(2,1)S(1)}, u32[]{:S(2)}, u32[]{:S(2)}) collective-permute-start(bf16[2080,128]{1,0:T(8,128)(2,1)} %panel_and_gains.1), channel_id=1, source_target_pairs={{0,1},{1,2},{2,3},{3,0},{4,5},{5,6},{6,7},{7,4},{8,9},{9,10},{10,1... | collective-permute-start | bytes 1597448 | tf_op jit(solution)/shard_map/ppermute | solution.py:642
  5.8 47.9 %collective-permute-start.31 = (bf16[2080,128]{1,0:T(8,128)(2,1)}, bf16[2080,128]{1,0:T(8,128)(2,1)S(1)}, u32[]{:S(2)}, u32[]{:S(2)}) collective-permute-start(bf16[2080,128]{1,0:T(8,128)(2,1)} %panel_and_gains.1), channel_id=1, source_target_pairs={{0,2},{1,3},{2,0},{3,1},{4,6},{5,7},{6,4},{7,5},{8,10},{9,11},{10,... | collective-permute-start | bytes 1597448 | tf_op jit(solution)/shard_map/ppermute | solution.py:642
  7.3 46.4 %collective-permute-start.30 = (bf16[2080,128]{1,0:T(8,128)(2,1)}, bf16[2080,128]{1,0:T(8,128)(2,1)S(1)}, u32[]{:S(2)}, u32[]{:S(2)}) collective-permute-start(bf16[2080,128]{1,0:T(8,128)(2,1)} %panel_and_gains.1), channel_id=1, source_target_pairs={{0,3},{1,0},{2,1},{3,2},{4,7},{5,4},{6,5},{7,6},{8,11},{9,8},{10,9... | collective-permute-start | bytes 1597448 | tf_op jit(solution)/shard_map/ppermute | solution.py:642
  8.8 17.8 %collective-permute-start.28 = (bf16[2080,128]{1,0:T(8,128)(2,1)}, bf16[2080,128]{1,0:T(8,128)(2,1)}, u32[]{:S(2)}, u32[]{:S(2)}) collective-permute-start(bf16[2080,128]{1,0:T(8,128)(2,1)} %panel_and_gains.1), channel_id=1, source_target_pairs={{0,8},{8,0},{16,24},{24,16},{1,9},{9,1},{17,25},{25,17},{2,10},{10... | collective-permute-start | bytes 1597448 | tf_op jit(solution)/shard_map/ppermute | solution.py:646
  10.3 16.2 %collective-permute-start.29 = (s32[62]{0:T(128)S(1)}, s32[62]{0:T(128)S(1)}, u32[]{:S(2)}, u32[]{:S(2)}) collective-permute-start(s32[62]{0:T(128)S(1)} %bitcast.98), channel_id=1, source_target_pairs={{0,8},{8,0},{16,24},{24,16},{1,9},{9,1},{17,25},{25,17},{2,10},{10... | collective-permute-start | bytes 752 | tf_op jit(solution)/shard_map/ppermute | solution.py:647
  26.6 3.6 %collective-permute-start.33 = (s32[3]{0:T(128)S(1)}, s32[3]{0:T(128)S(1)}, u32[]{:S(2)}, u32[]{:S(2)}) collective-permute-start(s32[3]{0:T(128)S(1)} %add_convert_fusion), channel_id=1, source_target_pairs={{0,8},{8,0},{16,24},{24,16},{1,9},{9,1},{17,25},{25,17},{2,10},{10... | collective-permute-start | bytes 44 | tf_op jit(solution)/shard_map/ppermute | solution.py:665
  31.4 22.3 %collective-permute-start.36 = (bf16[2080,128]{1,0:T(8,128)(2,1)}, bf16[2080,128]{1,0:T(8,128)(2,1)}, u32[]{:S(2)}, u32[]{:S(2)}) collective-permute-start(bf16[2080,128]{1,0:T(8,128)(2,1)} %dynamic_update_slice.3), channel_id=1, source_target_pairs={{0,1},{1,2},{2,3},{3,0},{4,5},{5,6},{6,7},{7,4},{8,9},{9,10},{10,1... | collective-permute-start | bytes 1597448 | tf_op jit(solution)/shard_map/ppermute | solution.py:642
  32.0 23.0 %collective-permute-start.35 = (bf16[2080,128]{1,0:T(8,128)(2,1)}, bf16[2080,128]{1,0:T(8,128)(2,1)}, u32[]{:S(2)}, u32[]{:S(2)}) collective-permute-start(bf16[2080,128]{1,0:T(8,128)(2,1)} %dynamic_update_slice.3), channel_id=1, source_target_pairs={{0,2},{1,3},{2,0},{3,1},{4,6},{5,7},{6,4},{7,5},{8,10},{9,11},{10,... | collective-permute-start | bytes 1597448 | tf_op jit(solution)/shard_map/ppermute | solution.py:642
  32.5 22.5 %collective-permute-start.34 = (bf16[2080,128]{1,0:T(8,128)(2,1)}, bf16[2080,128]{1,0:T(8,128)(2,1)}, u32[]{:S(2)}, u32[]{:S(2)}) collective-permute-start(bf16[2080,128]{1,0:T(8,128)(2,1)} %dynamic_update_slice.3), channel_id=1, source_target_pairs={{0,3},{1,0},{2,1},{3,2},{4,7},{5,4},{6,5},{7,6},{8,11},{9,8},{10,9... | collective-permute-start | bytes 1597448 | tf_op jit(solution)/shard_map/ppermute | solution.py:642
  34.6 20.5 %copy-start.2 = (bf16[2080,128]{1,0:T(8,128)(2,1)S(1)}, bf16[2080,128]{1,0:T(8,128)(2,1)}, u32[]{:S(2)}) copy-start(bf16[2080,128]{1,0:T(8,128)(2,1)} %panel_and_gains.1) | copy-start | bytes 1597444
  58.4 4.9 %copy-start = (bf16[4,2,2080,128]{3,2,1,0:T(8,128)(2,1)}, bf16[4,2,2080,128]{3,2,1,0:T(8,128)(2,1)S(1)}, u32[]{:S(2)}) copy-start(bf16[4,2,2080,128]{3,2,1,0:T(8,128)(2,1)S(1)} %pad_maximum_fusion.4.mine_ref) | copy-start | bytes 12779524
  58.5 7.5 %collective-permute-start.37 = (bf16[4,2,2080,128]{3,2,1,0:T(8,128)(2,1)S(1)}, bf16[4,2,2080,128]{3,2,1,0:T(8,128)(2,1)}, u32[]{:S(2)}, u32[]{:S(2)}) collective-permute-start(bf16[4,2,2080,128]{3,2,1,0:T(8,128)(2,1)S(1)} %pad_maximum_fusion.4.mine_ref), channel_id=1, source_target_pairs={{0,4},{4,0},{1,5},{5,1},{2,6},{6,2},{3,7},{7,3},{8,12},{12,8},{9,1... | collective-permute-start | bytes 12779528 | tf_op jit(solution)/shard_map/ppermute | solution.py:682
  58.5 94.2 %collective-permute-start.38 = (bf16[65,128,128]{2,1,0:T(8,128)(2,1)}, bf16[65,128,128]{2,1,0:T(8,128)(2,1)}, u32[]{:S(2)}, u32[]{:S(2)}) collective-permute-start(bf16[65,128,128]{2,1,0:T(8,128)(2,1)} %get-tuple-element.238), channel_id=1, source_target_pairs={{0,3},{1,0},{2,1},{3,2},{4,7},{5,4},{6,5},{7,6},{8,11},{9,8},{10,9... | collective-permute-start | bytes 6389768 | tf_op jit(solution)/shard_map/ppermute | solution.py:679
  60.9 91.8 %collective-permute-start.39 = (bf16[65,128,128]{2,1,0:T(8,128)(2,1)}, bf16[65,128,128]{2,1,0:T(8,128)(2,1)}, u32[]{:S(2)}, u32[]{:S(2)}) collective-permute-start(bf16[65,128,128]{2,1,0:T(8,128)(2,1)} %get-tuple-element.239), channel_id=1, source_target_pairs={{0,8},{8,0},{16,24},{24,16},{1,9},{9,1},{17,25},{25,17},{2,10},{10... | collective-permute-start | bytes 6389768 | tf_op jit(solution)/shard_map/ppermute | solution.py:678
  62.5 91.9 %collective-permute-start.40 = (bf16[65,128,128]{2,1,0:T(8,128)(2,1)}, bf16[65,128,128]{2,1,0:T(8,128)(2,1)}, u32[]{:S(2)}, u32[]{:S(2)}) collective-permute-start(bf16[65,128,128]{2,1,0:T(8,128)(2,1)} %get-tuple-element.240), channel_id=1, source_target_pairs={{0,11},{1,8},{2,9},{3,10},{8,3},{9,0},{10,1},{11,2},{16,27},{17,24... | collective-permute-start | bytes 6389768 | tf_op jit(solution)/shard_map/ppermute | solution.py:677
  156.4 4.6 %collective-permute-start = (bf16[65,128,128]{2,1,0:T(8,128)(2,1)}, bf16[65,128,128]{2,1,0:T(8,128)(2,1)}, u32[]{:S(2)}, u32[]{:S(2)}) collective-permute-start(bf16[65,128,128]{2,1,0:T(8,128)(2,1)} %get-tuple-element.93), channel_id=1, source_target_pairs={{0,4},{4,0},{1,5},{5,1},{2,6},{6,2},{3,7},{7,3},{8,12},{12,8},{9,1... | collective-permute-start | bytes 6389768 | tf_op jit(solution)/shard_map/cond/branch_0_fun/ppermute | solution.py:701
  156.5 7.6 %collective-permute-start.1 = (bf16[65,128,128]{2,1,0:T(8,128)(2,1)}, bf16[65,128,128]{2,1,0:T(8,128)(2,1)}, u32[]{:S(2)}, u32[]{:S(2)}) collective-permute-start(bf16[65,128,128]{2,1,0:T(8,128)(2,1)} %get-tuple-element.94), channel_id=1, source_target_pairs={{0,4},{4,0},{1,5},{5,1},{2,6},{6,2},{3,7},{7,3},{8,12},{12,8},{9,1... | collective-permute-start | bytes 6389768 | tf_op jit(solution)/shard_map/cond/branch_0_fun/ppermute | solution.py:701
  157.0 10.1 %collective-permute-start.2 = (bf16[65,128,128]{2,1,0:T(8,128)(2,1)}, bf16[65,128,128]{2,1,0:T(8,128)(2,1)}, u32[]{:S(2)}, u32[]{:S(2)}) collective-permute-start(bf16[65,128,128]{2,1,0:T(8,128)(2,1)} %get-tuple-element.112), channel_id=1, source_target_pairs={{0,4},{4,0},{1,5},{5,1},{2,6},{6,2},{3,7},{7,3},{8,12},{12,8},{9,1... | collective-permute-start | bytes 6389768 | tf_op jit(solution)/shard_map/cond/branch_0_fun/ppermute | solution.py:701
  167.1 5.2 %collective-permute-start.41 = (bf16[81,128,128]{2,1,0:T(8,128)(2,1)}, bf16[81,128,128]{2,1,0:T(8,128)(2,1)S(1)}, u32[]{:S(2)}, u32[]{:S(2)}) collective-permute-start(bf16[81,128,128]{2,1,0:T(8,128)(2,1)} %get-tuple-element.245), channel_id=1, source_target_pairs={{0,4},{4,0},{1,5},{5,1},{2,6},{6,2},{3,7},{7,3},{8,12},{12,8},{9,1... | collective-permute-start | bytes 7962632 | tf_op jit(solution)/shard_map/ppermute | solution.py:680
  172.3 1.5 copy-start.1
